TPU v7x, 1024 devices: a whole 4x8x16 slice. The times are simulated.
1024 devices in a mesh: gx: 16 (over x, z_lo), gy: 4 (over z_hi), gz: 16 (over y, core).
Axes of the slice: x: 4, y: 8, z: 16 (z_hi: 4, z_lo: 4; z = z_hi * 4 + z_lo), core: 2. Of those that a mesh axis runs over, the one named last changes fastest.
Arguments:
- vel_x: float32 [256, 128, 512], P('gx', 'gz', 'gy'), may hold values from -6 to 6
- vel_y: float32 [256, 128, 512], P('gx', 'gz', 'gy'), may hold values from -6 to 6
- vel_z: float32 [256, 128, 512], P('gx', 'gz', 'gy'), may hold values from -6 to 6
- pressure: float32 [256, 128, 512], P('gx', 'gz', 'gy'), may hold values from -6 to 6
- phase: int32 [256, 128, 512], P('gx', 'gz', 'gy'), may hold values from 0 to 3
- visc_scale: float32 [4], replicated, may hold values from 0.5 to 2
- power_n: float32 [4], replicated, may hold values from 1 to 4
- density: float32 [4], replicated, may hold values from 0.5 to 1.5
Outputs:
- out_vx: float32 [256, 128, 512], P('gx', 'gz', 'gy')
- out_vy: float32 [256, 128, 512], P('gx', 'gz', 'gy')
- out_vz: float32 [256, 128, 512], P('gx', 'gz', 'gy')
- out_p: float32 [256, 128, 512], P('gx', 'gz', 'gy')
- out_eta: float32 [256, 128, 512], P('gx', 'gz', 'gy')
All inputs are finite; a program needn't handle non-finite values.
Results may differ from a plain program's by a relative error of at most 0.00013.
Values sent between devices are 32-bit elements; how exact they have to be, the bound alone decides.
A program may use at most 32 MiB of HBM per device.

v0:
```python
import jax
import jax.numpy as jnp
from jax import lax
from jax.sharding import PartitionSpec as P

ITERS = 4
PHASES = 4


strain_floor = 1.0
pressure_step = 0.5
velocity_step = 0.1


def padded_2(block, sides, width):
    for axis, dim in sides:
        count = lax.axis_size(axis)
        forward = [(i, i + 1) for i in range(count - 1)]
        backward = [(target, source) for source, target in forward]
        low = lax.ppermute(
            lax.slice_in_dim(block, block.shape[dim] - width, None, axis=dim), axis, forward
        )
        high = lax.ppermute(lax.slice_in_dim(block, 0, width, axis=dim), axis, backward)
        block = jnp.concatenate([low, block, high], axis=dim)
    return block


def lookup(phase, table):
    out = jnp.zeros(phase.shape, jnp.float32)
    for index in range(PHASES):
        out = out + jnp.where(phase == index, table[index], jnp.float32(0.0))
    return out


def strain_rate_list(padded):
    strain_rate_first = padded[0, 2:, 1:-1, 1:-1] - padded[0, 1:-1, 1:-1, 1:-1]
    strain_rate_second = padded[1, 1:-1, 2:, 1:-1] - padded[1, 1:-1, 1:-1, 1:-1]
    strain_rate_third = padded[2, 1:-1, 1:-1, 2:] - padded[2, 1:-1, 1:-1, 1:-1]
    return (strain_rate_first, strain_rate_second, strain_rate_third)


def viscosity(strain_rate_first, strain_rate_second, strain_rate_third, prefactor, exponent):
    div = strain_rate_first + strain_rate_second + strain_rate_third
    third = div / 3.0
    inv = (
        0.5
        * (
            (strain_rate_first - third) ** 2
            + (strain_rate_second - third) ** 2
            + (strain_rate_third - third) ** 2
        )
        + strain_floor
    )
    eta = prefactor * jnp.exp(0.5 * (1.0 / exponent - 1.0) * jnp.log(inv))
    return (eta, div)


def slice_along(field, offset, grid_extent):
    return field[
        1 + offset[0] : 1 + offset[0] + grid_extent[0],
        1 + offset[1] : 1 + offset[1] + grid_extent[1],
        1 + offset[2] : 1 + offset[2] + grid_extent[2],
    ]


def unit(sweep_heading, sign):
    offset = [0, 0, 0]
    offset[sweep_heading] = sign
    return tuple(offset)


def joined(first, second):
    return tuple((first[n] + second[n] for n in range(3)))


def residual_field(sweep_heading, padded_velocity, padded_pressure, padded_viscosity, grid_extent):
    zero_scalar = (0, 0, 0)
    backward_neighbor = unit(sweep_heading, -1)
    middle_slice = slice_along(padded_velocity, zero_scalar, grid_extent)
    viscosity_current = slice_along(padded_viscosity, zero_scalar, grid_extent)
    viscosity_backward = slice_along(padded_viscosity, backward_neighbor, grid_extent)
    momentum_residual = -(
        slice_along(padded_pressure, zero_scalar, grid_extent)
        - slice_along(padded_pressure, backward_neighbor, grid_extent)
    )
    for other in range(3):
        upper_neighbor = unit(other, 1)
        lower_neighbor = unit(other, -1)
        if other == sweep_heading:
            momentum_residual = (
                momentum_residual
                + viscosity_current
                * (slice_along(padded_velocity, upper_neighbor, grid_extent) - middle_slice)
                - viscosity_backward
                * (middle_slice - slice_along(padded_velocity, backward_neighbor, grid_extent))
            )
        else:
            viscosity_above = 0.25 * (
                viscosity_current
                + viscosity_backward
                + slice_along(padded_viscosity, upper_neighbor, grid_extent)
                + slice_along(
                    padded_viscosity, joined(backward_neighbor, upper_neighbor), grid_extent
                )
            )
            viscosity_below = 0.25 * (
                viscosity_current
                + viscosity_backward
                + slice_along(padded_viscosity, lower_neighbor, grid_extent)
                + slice_along(
                    padded_viscosity, joined(backward_neighbor, lower_neighbor), grid_extent
                )
            )
            momentum_residual = (
                momentum_residual
                + viscosity_above
                * (slice_along(padded_velocity, upper_neighbor, grid_extent) - middle_slice)
                - viscosity_below
                * (middle_slice - slice_along(padded_velocity, lower_neighbor, grid_extent))
            )
    return (momentum_residual, 0.5 * (viscosity_current + viscosity_backward))


def pressure_sum(values):
    return lax.psum(jnp.sum(values), ("gx", "gy", "gz"))


def local(vel_x, vel_y, vel_z, pressure, phase, visc_scale, power_n, density):
    grid_extent = pressure.shape
    counts = (lax.axis_size("gx"), lax.axis_size("gz"), lax.axis_size("gy"))
    starts = (
        lax.axis_index("gx") * grid_extent[0],
        lax.axis_index("gz") * grid_extent[1],
        lax.axis_index("gy") * grid_extent[2],
    )

    def coord(sweep_heading, extra):
        length = grid_extent[sweep_heading] + 2 * extra
        index = starts[sweep_heading] - extra + lax.iota(jnp.int32, length)
        dims = [1, 1, 1]
        dims[sweep_heading] = length
        return index.reshape(dims)

    velocity = [
        jnp.where(coord(axis_number, 0) == 0, jnp.float32(0.0), v)
        for axis_number, v in enumerate((vel_x, vel_z, vel_y))
    ]
    rho = lookup(phase, density)
    total_cells = float(
        grid_extent[0] * grid_extent[1] * grid_extent[2] * counts[0] * counts[1] * counts[2]
    )
    inside = jnp.ones((1, 1, 1), jnp.bool_)
    for axis_number in range(3):
        place = coord(axis_number, 1)
        inside = inside & (place >= 0) & (place < grid_extent[axis_number] * counts[axis_number])
    prefactor = lookup(phase, visc_scale)
    exponent = lookup(phase, power_n)
    eta = prefactor
    for step in range(ITERS):
        stacked_rates = jnp.stack(velocity)
        padded_velocity = padded_2(stacked_rates, (("gx", 1), ("gy", 3), ("gz", 2)), 1)
        strain_rate_first, strain_rate_second, strain_rate_third = strain_rate_list(padded_velocity)
        eta, div = viscosity(
            strain_rate_first, strain_rate_second, strain_rate_third, prefactor, exponent
        )
        pressure = pressure - pressure_step * eta * div
        pressure = pressure - pressure_sum(pressure) / total_cells
        both = padded_2(jnp.stack([pressure, eta]), (("gx", 1), ("gy", 3), ("gz", 2)), 1)
        padded_pressure = both[0]
        padded_viscosity = both[1]
        updated = []
        for axis_number in range(3):
            momentum_residual, face_slice = residual_field(
                axis_number,
                padded_velocity[axis_number],
                padded_pressure,
                padded_viscosity,
                grid_extent,
            )
            if axis_number == 1:
                momentum_residual = momentum_residual - rho
            fresh = velocity[axis_number] + velocity_step * momentum_residual / face_slice
            updated.append(jnp.where(coord(axis_number, 0) == 0, jnp.float32(0.0), fresh))
        velocity = updated
    return (velocity[0], velocity[2], velocity[1], pressure, eta)


def solution(mesh):
    return jax.shard_map(
        local,
        mesh=mesh,
        in_specs=(
            P("gx", "gz", "gy"),
            P("gx", "gz", "gy"),
            P("gx", "gz", "gy"),
            P("gx", "gz", "gy"),
            P("gx", "gz", "gy"),
            P(),
            P(),
            P(),
        ),
        out_specs=(
            P("gx", "gz", "gy"),
            P("gx", "gz", "gy"),
            P("gx", "gz", "gy"),
            P("gx", "gz", "gy"),
            P("gx", "gz", "gy"),
        ),
        check_vma=False,
    )
```

profile of v0, /device:TPU:1, one launch (start us, length us, event | category | flops | bytes accessed | tf_op | source)
XLA Modules:
  0.0 875.3 jit_solution(4260130216798516460)
XLA Ops:
  3.1 5.5 collective-permute-start.1
  10.8 11.3 %collective-permute-start.2 = (f32[3,18,8,1]{3,2,1,0:T(8,128)S(1)}, f32[3,18,8,1]{3,2,1,0:T(8,128)S(1)}, u32[]{:S(2)}, u32[]{:S(2)}) collective-permute-start(f32[3,18,8,1]{3,2,1,0:T(8,128)S(1)} %get-tuple-element.71), channel_id=1, source_target_pairs={{0,16},{16,32},{32,48},{1,17},{17,33},{33,49},{2,18},{18,34},{34,5... | collective-permute-start | bytes 5192 | tf_op jit(solution)/shard_map/ppermute | solution.py:20
  22.7 5.5 collective-permute-done.3
  28.6 10.3 %collective-permute-start.4 = (f32[3,18,1,130]{3,2,1,0:T(1,128)S(1)}, f32[3,18,1,130]{3,2,1,0:T(1,128)S(1)}, u32[]{:S(2)}, u32[]{:S(2)}) collective-permute-start(f32[3,18,1,130]{3,2,1,0:T(1,128)S(1)} %get-tuple-element.46), channel_id=1, source_target_pairs={{1,0},{2,1},{3,2},{4,3},{5,4},{6,5},{7,6},{8,7},{9,8},{10,9},{11,1... | collective-permute-start | bytes 84248 | tf_op jit(solution)/shard_map/ppermute | solution.py:23
  41.3 5.9 fusion.286
  47.2 136.8 %psum.28 = f32[]{:T(128)} all-reduce(f32[]{:T(128)} %get-tuple-element.18), channel_id=1, replica_groups=mesh['gx'=16,'gy'=4,'gz'=16] {'gx','gy','gz'}, use_global_device_ids=true, to_apply=%region_1.2 | all-reduce | flops 1 | bytes 8 | tf_op jit(solution)/shard_map/psum | solution.py:125
  199.6 7.9 collective-permute-start.7
  211.8 10.2 %collective-permute-start.10 = (f32[2,18,1,130]{3,2,1,0:T(1,128)S(1)}, f32[2,18,1,130]{3,2,1,0:T(1,128)S(1)}, u32[]{:S(2)}, u32[]{:S(2)}) collective-permute-start(f32[2,18,1,130]{3,2,1,0:T(1,128)S(1)} %get-tuple-element.64), channel_id=1, source_target_pairs={{1,0},{2,1},{3,2},{4,3},{5,4},{6,5},{7,6},{8,7},{9,8},{10,9},{11,1... | collective-permute-start | bytes 56168 | tf_op jit(solution)/shard_map/ppermute | solution.py:23
  236.6 7.9 collective-permute-start.14
  248.5 7.6 collective-permute-start.16
  258.9 6.0 fusion.283
  264.9 135.9 %psum.29 = f32[]{:T(128)} all-reduce(f32[]{:T(128)} %get-tuple-element.13), channel_id=1, replica_groups=mesh['gx'=16,'gy'=4,'gz'=16] {'gx','gy','gz'}, use_global_device_ids=true, to_apply=%region_3.4 | all-reduce | flops 1 | bytes 8 | tf_op jit(solution)/shard_map/psum | solution.py:125
  417.5 7.9 collective-permute-start.19
  441.8 7.6 collective-permute-start.25
  451.7 7.9 collective-permute-start.26
  471.2 6.0 fusion.280
  477.1 143.6 %psum.30 = f32[]{:T(128)} all-reduce(f32[]{:T(128)} %get-tuple-element.8), channel_id=1, replica_groups=mesh['gx'=16,'gy'=4,'gz'=16] {'gx','gy','gz'}, use_global_device_ids=true, to_apply=%region_5.6 | all-reduce | flops 1 | bytes 8 | tf_op jit(solution)/shard_map/psum | solution.py:125
  637.1 8.1 collective-permute-start.31
  645.6 7.3 collective-permute-done.32
  671.3 7.9 collective-permute-start.38
  679.2 8.6 collective-permute-done.39
  694.6 5.9 fusion.279
  700.5 140.0 %psum.31 = f32[]{:T(128)} all-reduce(f32[]{:T(128)} %get-tuple-element.5), channel_id=1, replica_groups=mesh['gx'=16,'gy'=4,'gz'=16] {'gx','gy','gz'}, use_global_device_ids=true, to_apply=%region_7.8 | all-reduce | flops 1 | bytes 8 | tf_op jit(solution)/shard_map/psum | solution.py:125
  849.0 7.9 collective-permute-start.43
  (175 shorter events, 161.7 us)
Async XLA Ops:
  9.5 18.7 %collective-permute-start.3 = (f32[3,18,8,1]{3,2,1,0:T(8,128)S(1)}, f32[3,18,8,1]{3,2,1,0:T(8,128)S(1)}, u32[]{:S(2)}, u32[]{:S(2)}) collective-permute-start(f32[3,18,8,1]{3,2,1,0:T(8,128)S(1)} %get-tuple-element.72), channel_id=1, source_target_pairs={{16,0},{32,16},{48,32},{17,1},{33,17},{49,33},{18,2},{34,18},{50,3... | collective-permute-start | bytes 5192 | tf_op jit(solution)/shard_map/ppermute | solution.py:23
  10.8 17.4 %collective-permute-start.2 = (f32[3,18,8,1]{3,2,1,0:T(8,128)S(1)}, f32[3,18,8,1]{3,2,1,0:T(8,128)S(1)}, u32[]{:S(2)}, u32[]{:S(2)}) collective-permute-start(f32[3,18,8,1]{3,2,1,0:T(8,128)S(1)} %get-tuple-element.71), channel_id=1, source_target_pairs={{0,16},{16,32},{32,48},{1,17},{17,33},{33,49},{2,18},{18,34},{34,5... | collective-permute-start | bytes 5192 | tf_op jit(solution)/shard_map/ppermute | solution.py:20
  28.6 12.7 %collective-permute-start.4 = (f32[3,18,1,130]{3,2,1,0:T(1,128)S(1)}, f32[3,18,1,130]{3,2,1,0:T(1,128)S(1)}, u32[]{:S(2)}, u32[]{:S(2)}) collective-permute-start(f32[3,18,1,130]{3,2,1,0:T(1,128)S(1)} %get-tuple-element.46), channel_id=1, source_target_pairs={{1,0},{2,1},{3,2},{4,3},{5,4},{6,5},{7,6},{8,7},{9,8},{10,9},{11,1... | collective-permute-start | bytes 84248 | tf_op jit(solution)/shard_map/ppermute | solution.py:23
  196.2 11.3 %collective-permute-start.11 = (f32[3,18,1,130]{3,2,1,0:T(1,128)S(1)}, f32[3,18,1,130]{3,2,1,0:T(1,128)S(1)}, u32[]{:S(2)}, u32[]{:S(2)}) collective-permute-start(f32[3,18,1,130]{3,2,1,0:T(1,128)S(1)} %get-tuple-element.45), channel_id=1, source_target_pairs={{0,1},{1,2},{2,3},{3,4},{4,5},{5,6},{6,7},{7,8},{8,9},{9,10},{10,1... | collective-permute-start | bytes 84248 | tf_op jit(solution)/shard_map/ppermute | solution.py:20
  198.3 13.2 %collective-permute-start.8 = (f32[2,18,8,1]{3,2,1,0:T(8,128)S(1)}, f32[2,18,8,1]{3,2,1,0:T(8,128)S(1)}, u32[]{:S(2)}, u32[]{:S(2)}) collective-permute-start(f32[2,18,8,1]{3,2,1,0:T(8,128)S(1)} %get-tuple-element.88), channel_id=1, source_target_pairs={{16,0},{32,16},{48,32},{17,1},{33,17},{49,33},{18,2},{34,18},{50,3... | collective-permute-start | bytes 3464 | tf_op jit(solution)/shard_map/ppermute | solution.py:23
  199.6 11.9 %collective-permute-start.7 = (f32[2,18,8,1]{3,2,1,0:T(8,128)S(1)}, f32[2,18,8,1]{3,2,1,0:T(8,128)S(1)}, u32[]{:S(2)}, u32[]{:S(2)}) collective-permute-start(f32[2,18,8,1]{3,2,1,0:T(8,128)S(1)} %get-tuple-element.87), channel_id=1, source_target_pairs={{0,16},{16,32},{32,48},{1,17},{17,33},{33,49},{2,18},{18,34},{34,5... | collective-permute-start | bytes 3464 | tf_op jit(solution)/shard_map/ppermute | solution.py:20
  211.8 12.3 %collective-permute-start.10 = (f32[2,18,1,130]{3,2,1,0:T(1,128)S(1)}, f32[2,18,1,130]{3,2,1,0:T(1,128)S(1)}, u32[]{:S(2)}, u32[]{:S(2)}) collective-permute-start(f32[2,18,1,130]{3,2,1,0:T(1,128)S(1)} %get-tuple-element.64), channel_id=1, source_target_pairs={{1,0},{2,1},{3,2},{4,3},{5,4},{6,5},{7,6},{8,7},{9,8},{10,9},{11,1... | collective-permute-start | bytes 56168 | tf_op jit(solution)/shard_map/ppermute | solution.py:23
  235.3 12.7 %collective-permute-start.15 = (f32[3,18,8,1]{3,2,1,0:T(8,128)S(1)}, f32[3,18,8,1]{3,2,1,0:T(8,128)S(1)}, u32[]{:S(2)}, u32[]{:S(2)}) collective-permute-start(f32[3,18,8,1]{3,2,1,0:T(8,128)S(1)} %get-tuple-element.70), channel_id=1, source_target_pairs={{16,0},{32,16},{48,32},{17,1},{33,17},{49,33},{18,2},{34,18},{50,3... | collective-permute-start | bytes 5192 | tf_op jit(solution)/shard_map/ppermute | solution.py:23
  236.6 11.4 %collective-permute-start.14 = (f32[3,18,8,1]{3,2,1,0:T(8,128)S(1)}, f32[3,18,8,1]{3,2,1,0:T(8,128)S(1)}, u32[]{:S(2)}, u32[]{:S(2)}) collective-permute-start(f32[3,18,8,1]{3,2,1,0:T(8,128)S(1)} %get-tuple-element.69), channel_id=1, source_target_pairs={{0,16},{16,32},{32,48},{1,17},{17,33},{33,49},{2,18},{18,34},{34,5... | collective-permute-start | bytes 5192 | tf_op jit(solution)/shard_map/ppermute | solution.py:20
  248.5 10.5 %collective-permute-start.16 = (f32[3,18,1,130]{3,2,1,0:T(1,128)S(1)}, f32[3,18,1,130]{3,2,1,0:T(1,128)S(1)}, u32[]{:S(2)}, u32[]{:S(2)}) collective-permute-start(f32[3,18,1,130]{3,2,1,0:T(1,128)S(1)} %get-tuple-element.44), channel_id=1, source_target_pairs={{1,0},{2,1},{3,2},{4,3},{5,4},{6,5},{7,6},{8,7},{9,8},{10,9},{11,1... | collective-permute-start | bytes 84248 | tf_op jit(solution)/shard_map/ppermute | solution.py:23
  412.2 13.2 %collective-permute-start.23 = (f32[3,18,1,130]{3,2,1,0:T(1,128)S(1)}, f32[3,18,1,130]{3,2,1,0:T(1,128)S(1)}, u32[]{:S(2)}, u32[]{:S(2)}) collective-permute-start(f32[3,18,1,130]{3,2,1,0:T(1,128)S(1)} %get-tuple-element.43), channel_id=1, source_target_pairs={{0,1},{1,2},{2,3},{3,4},{4,5},{5,6},{6,7},{7,8},{8,9},{9,10},{10,1... | collective-permute-start | bytes 84248 | tf_op jit(solution)/shard_map/ppermute | solution.py:20
  416.2 13.5 %collective-permute-start.20 = (f32[2,18,8,1]{3,2,1,0:T(8,128)S(1)}, f32[2,18,8,1]{3,2,1,0:T(8,128)S(1)}, u32[]{:S(2)}, u32[]{:S(2)}) collective-permute-start(f32[2,18,8,1]{3,2,1,0:T(8,128)S(1)} %get-tuple-element.86), channel_id=1, source_target_pairs={{16,0},{32,16},{48,32},{17,1},{33,17},{49,33},{18,2},{34,18},{50,3... | collective-permute-start | bytes 3464 | tf_op jit(solution)/shard_map/ppermute | solution.py:23
  417.5 12.2 %collective-permute-start.19 = (f32[2,18,8,1]{3,2,1,0:T(8,128)S(1)}, f32[2,18,8,1]{3,2,1,0:T(8,128)S(1)}, u32[]{:S(2)}, u32[]{:S(2)}) collective-permute-start(f32[2,18,8,1]{3,2,1,0:T(8,128)S(1)} %get-tuple-element.85), channel_id=1, source_target_pairs={{0,16},{16,32},{32,48},{1,17},{17,33},{33,49},{2,18},{18,34},{34,5... | collective-permute-start | bytes 3464 | tf_op jit(solution)/shard_map/ppermute | solution.py:20
  450.4 14.3 %collective-permute-start.27 = (f32[3,18,8,1]{3,2,1,0:T(8,128)S(1)}, f32[3,18,8,1]{3,2,1,0:T(8,128)S(1)}, u32[]{:S(2)}, u32[]{:S(2)}) collective-permute-start(f32[3,18,8,1]{3,2,1,0:T(8,128)S(1)} %get-tuple-element.68), channel_id=1, source_target_pairs={{16,0},{32,16},{48,32},{17,1},{33,17},{49,33},{18,2},{34,18},{50,3... | collective-permute-start | bytes 5192 | tf_op jit(solution)/shard_map/ppermute | solution.py:23
  451.7 13.0 %collective-permute-start.26 = (f32[3,18,8,1]{3,2,1,0:T(8,128)S(1)}, f32[3,18,8,1]{3,2,1,0:T(8,128)S(1)}, u32[]{:S(2)}, u32[]{:S(2)}) collective-permute-start(f32[3,18,8,1]{3,2,1,0:T(8,128)S(1)} %get-tuple-element.67), channel_id=1, source_target_pairs={{0,16},{16,32},{32,48},{1,17},{17,33},{33,49},{2,18},{18,34},{34,5... | collective-permute-start | bytes 5192 | tf_op jit(solution)/shard_map/ppermute | solution.py:20
  632.1 13.1 %collective-permute-start.35 = (f32[3,18,1,130]{3,2,1,0:T(1,128)S(1)}, f32[3,18,1,130]{3,2,1,0:T(1,128)S(1)}, u32[]{:S(2)}, u32[]{:S(2)}) collective-permute-start(f32[3,18,1,130]{3,2,1,0:T(1,128)S(1)} %get-tuple-element.41), channel_id=1, source_target_pairs={{0,1},{1,2},{2,3},{3,4},{4,5},{5,6},{6,7},{7,8},{8,9},{9,10},{10,1... | collective-permute-start | bytes 84248 | tf_op jit(solution)/shard_map/ppermute | solution.py:20
  635.8 17.1 %collective-permute-start.32 = (f32[2,18,8,1]{3,2,1,0:T(8,128)S(1)}, f32[2,18,8,1]{3,2,1,0:T(8,128)S(1)}, u32[]{:S(2)}, u32[]{:S(2)}) collective-permute-start(f32[2,18,8,1]{3,2,1,0:T(8,128)S(1)} %get-tuple-element.84), channel_id=1, source_target_pairs={{16,0},{32,16},{48,32},{17,1},{33,17},{49,33},{18,2},{34,18},{50,3... | collective-permute-start | bytes 3464 | tf_op jit(solution)/shard_map/ppermute | solution.py:23
  637.1 15.8 %collective-permute-start.31 = (f32[2,18,8,1]{3,2,1,0:T(8,128)S(1)}, f32[2,18,8,1]{3,2,1,0:T(8,128)S(1)}, u32[]{:S(2)}, u32[]{:S(2)}) collective-permute-start(f32[2,18,8,1]{3,2,1,0:T(8,128)S(1)} %get-tuple-element.83), channel_id=1, source_target_pairs={{0,16},{16,32},{32,48},{1,17},{17,33},{33,49},{2,18},{18,34},{34,5... | collective-permute-start | bytes 3464 | tf_op jit(solution)/shard_map/ppermute | solution.py:20
  670.0 17.8 %collective-permute-start.39 = (f32[3,18,8,1]{3,2,1,0:T(8,128)S(1)}, f32[3,18,8,1]{3,2,1,0:T(8,128)S(1)}, u32[]{:S(2)}, u32[]{:S(2)}) collective-permute-start(f32[3,18,8,1]{3,2,1,0:T(8,128)S(1)} %get-tuple-element.66), channel_id=1, source_target_pairs={{16,0},{32,16},{48,32},{17,1},{33,17},{49,33},{18,2},{34,18},{50,3... | collective-permute-start | bytes 5192 | tf_op jit(solution)/shard_map/ppermute | solution.py:23
  671.3 16.5 %collective-permute-start.38 = (f32[3,18,8,1]{3,2,1,0:T(8,128)S(1)}, f32[3,18,8,1]{3,2,1,0:T(8,128)S(1)}, u32[]{:S(2)}, u32[]{:S(2)}) collective-permute-start(f32[3,18,8,1]{3,2,1,0:T(8,128)S(1)} %get-tuple-element.65), channel_id=1, source_target_pairs={{0,16},{16,32},{32,48},{1,17},{17,33},{33,49},{2,18},{18,34},{34,5... | collective-permute-start | bytes 5192 | tf_op jit(solution)/shard_map/ppermute | solution.py:20
  690.9 155.9 %collective-permute-start.47 = (f32[3,18,1,130]{3,2,1,0:T(1,128)S(1)}, f32[3,18,1,130]{3,2,1,0:T(1,128)S(1)}, u32[]{:S(2)}, u32[]{:S(2)}) collective-permute-start(f32[3,18,1,130]{3,2,1,0:T(1,128)S(1)} %get-tuple-element.39), channel_id=1, source_target_pairs={{0,1},{1,2},{2,3},{3,4},{4,5},{5,6},{6,7},{7,8},{8,9},{9,10},{10,1... | collective-permute-start | bytes 84248 | tf_op jit(solution)/shard_map/ppermute | solution.py:20
  847.7 11.4 %collective-permute-start.44 = (f32[2,18,8,1]{3,2,1,0:T(8,128)S(1)}, f32[2,18,8,1]{3,2,1,0:T(8,128)S(1)}, u32[]{:S(2)}, u32[]{:S(2)}) collective-permute-start(f32[2,18,8,1]{3,2,1,0:T(8,128)S(1)} %get-tuple-element.82), channel_id=1, source_target_pairs={{16,0},{32,16},{48,32},{17,1},{33,17},{49,33},{18,2},{34,18},{50,3... | collective-permute-start | bytes 3464 | tf_op jit(solution)/shard_map/ppermute | solution.py:23
  849.0 10.1 %collective-permute-start.43 = (f32[2,18,8,1]{3,2,1,0:T(8,128)S(1)}, f32[2,18,8,1]{3,2,1,0:T(8,128)S(1)}, u32[]{:S(2)}, u32[]{:S(2)}) collective-permute-start(f32[2,18,8,1]{3,2,1,0:T(8,128)S(1)} %get-tuple-element.81), channel_id=1, source_target_pairs={{0,16},{16,32},{32,48},{1,17},{17,33},{33,49},{2,18},{18,34},{34,5... | collective-permute-start | bytes 3464 | tf_op jit(solution)/shard_map/ppermute | solution.py:20
  859.4 9.8 %collective-permute-start.46 = (f32[2,18,1,130]{3,2,1,0:T(1,128)S(1)}, f32[2,18,1,130]{3,2,1,0:T(1,128)S(1)}, u32[]{:S(2)}, u32[]{:S(2)}) collective-permute-start(f32[2,18,1,130]{3,2,1,0:T(1,128)S(1)} %get-tuple-element.56), channel_id=1, source_target_pairs={{1,0},{2,1},{3,2},{4,3},{5,4},{6,5},{7,6},{8,7},{9,8},{10,9},{11,1... | collective-permute-start | bytes 56168 | tf_op jit(solution)/shard_map/ppermute | solution.py:23
  (33 other events, 392.0 us)
where the time goes:
time: 891 us; the launch traced here: 875 us
  blocking collectives  556 us (62%)
  starting transfers between devices  194 us (22%)
  other arithmetic  63.1 us (7%)
  waiting for transfers between devices  54.4 us (6%)
    psum x4, blocking collectives, pressure_sum(): return lax.psum(jnp.sum(values), ('gx', 'gy', 'gz'))  556 us
    ppermute x24, starting transfers between devices, padded_2(): lax.ppermute(lax.slice_in_dim(block, block.shape[dim] - width, None, axis...  132 us
    ppermute x24, starting transfers between devices, padded_2(): lax.ppermute(lax.slice_in_dim(block, 0, width, axis=dim), axis, backward)  62.6 us
    ppermute x24, waiting for transfers between devices, padded_2(): lax.ppermute(lax.slice_in_dim(block, 0, width, axis=dim), axis, backward)  47.4 us
    reduce_sum x4, other arithmetic, pressure_sum(): return lax.psum(jnp.sum(values), ('gx', 'gy', 'gz'))  23.7 us
  transfers between devices with their start and end apart: 48, of which 20 were waited for; matrix products, arithmetic and copies ran while one was open for 1% of the time, Pallas kernels for 0%

commit v1 on v0

v1 whole, which is shorter than its diff:
```python
import functools

import jax
import jax.numpy as jnp
from jax import lax
from jax.experimental import pallas as pl
from jax.experimental.pallas import tpu as pltpu
from jax.sharding import PartitionSpec as P

ITERS = 4
PHASES = 4
STRAIN_FLOOR = 1.0
PRESSURE_STEP = 0.5
VELOCITY_STEP = 0.1

BX, BZ, BY = 16, 8, 128
LOW, HIGH = 2, 4
YLOW, YHIGH = 4, 8
PLANES = BX + LOW + HIGH
ROWS = 2 * BZ
GROUP = YLOW + YHIGH
Z_LO = 4
MESH = pl.DeviceIdType.MESH

SIDES = tuple((a, b) for a in (-1, 0, 1) for b in (-1, 0, 1) if (a, b) != (0, 0))


def send_planes(a):
    return {0: (LOW, BX), 1: (LOW + BX - LOW, LOW), -1: (LOW, HIGH)}[a]


def land_planes(a):
    return {0: LOW, 1: 0, -1: LOW + BX}[a]


def send_rows(b):
    return {0: (0, BZ), 1: (BZ - LOW, LOW), -1: (0, HIGH)}[b]


def land_rows(b):
    return {0: 0, 1: ROWS - LOW, -1: BZ}[b]


def y_roll(x, s):
    r = pltpu.roll(x, s % BY, 1)
    swapped = jnp.concatenate([r[ROWS:], r[:ROWS]], axis=0)
    lane = lax.broadcasted_iota(jnp.int32, x.shape, 1)
    return jnp.where(lane == (0 if s == 1 else BY - 1), swapped, r)


def z_roll(x, s):
    return jnp.concatenate(
        [pltpu.roll(x[:ROWS], s % ROWS, 0), pltpu.roll(x[ROWS:], s % ROWS, 0)], axis=0
    )


def kernel(sizes, vx_ref, vy_ref, vz_ref, p_ref, ph_ref, vs_ref, pn_ref, dn_ref, out_ref,
           ph_in, first, second, s_pack, r_pack, vel, pres, pref, expo, rho, eta_out, ar_src, ar_buf,
           in_sem, ysend, yrecv, send_a, recv_a, send_b, recv_b, send_c, recv_c, ar_send, ar_recv):
    ngx, ngy, ngz, z_lo = sizes
    gx, gy, gz = lax.axis_index("gx"), lax.axis_index("gy"), lax.axis_index("gz")
    n_x, n_z = ngx // z_lo, z_lo * ngy

    in_copies = []
    for n, (src, dst) in enumerate(
        ((vx_ref, first.at[0, pl.ds(LOW, BX), pl.ds(0, BZ)]),
         (vz_ref, first.at[1, pl.ds(LOW, BX), pl.ds(0, BZ)]),
         (vy_ref, first.at[2, pl.ds(LOW, BX), pl.ds(0, BZ)]),
         (p_ref, first.at[3, pl.ds(LOW, BX), pl.ds(0, BZ)]),
         (ph_ref, ph_in))):
        cp = pltpu.make_async_copy(src, dst, in_sem.at[n])
        cp.start()
        in_copies.append(cp)

    def neighbour(a, b, c):
        return (lax.rem(gx + (a + ngx), ngx), lax.rem(gy + (c + ngy), ngy), lax.rem(gz + (b + ngz), ngz))

    def along_gz(o):
        return (gx, gy, lax.rem(gz + o, ngz))

    def along_x(o):
        return (lax.rem(gx + o * z_lo, ngx), gy, gz)

    z_here = gy * z_lo + lax.rem(gx, z_lo)

    def along_z(o):
        z = lax.rem(z_here + o, n_z)
        return (gx - lax.rem(gx, z_lo) + lax.rem(z, z_lo), z // z_lo, gz)

    sum_phases = (
        [along_gz(o) for o in range(1, ngz)],
        [along_x(o) for o in range(1, n_x)],
        [along_z(o) for o in range(1, n_z)],
    )

    barrier = pltpu.get_barrier_semaphore()
    greeted = [neighbour(a, b, 0) for a, b in SIDES] + [neighbour(0, 0, -1), neighbour(0, 0, 1)]
    greeted += [d for group in sum_phases for d in group]
    for d in greeted:
        pl.semaphore_signal(barrier, inc=1, device_id=d, device_id_type=MESH)

    lane_v = lax.broadcasted_iota(jnp.int32, (BZ, BY), 1)
    for cp in in_copies:
        cp.wait()
    first[4, LOW:LOW + BX, 0:BZ] = ph_in[...].astype(jnp.float32)

    def pack(k, carry):
        lo = jnp.zeros((BZ, BY), jnp.float32)
        hi = jnp.zeros((BZ, BY), jnp.float32)
        for q in range(2):
            for a in range(5):
                base = GROUP * a + 64 * q
                rolled = first[a, LOW + 2 * k + q, 0:BZ]
                if base:
                    rolled = pltpu.roll(rolled, base, 1)
                lo = jnp.where((lane_v >= base) & (lane_v < base + YHIGH), rolled, lo)
                if base:
                    hi = jnp.where((lane_v >= base - YLOW) & (lane_v < base), rolled, hi)
                else:
                    hi = jnp.where(lane_v >= BY - YLOW, rolled, hi)
        s_pack[0, k] = lo
        s_pack[1, k] = hi
        return carry

    lax.fori_loop(0, BX // 2, pack, 0)
    pl.semaphore_wait(barrier, len(greeted))

    y_copies = []
    for n, c in enumerate((-1, 1)):
        cp = pltpu.make_async_remote_copy(
            src_ref=s_pack.at[n], dst_ref=r_pack.at[n], send_sem=ysend.at[n], recv_sem=yrecv.at[n],
            device_id=neighbour(0, 0, c), device_id_type=MESH)
        cp.start()
        y_copies.append(cp)

    def exchange(buf, lo, count, send, recv):
        copies = []
        for n, (a, b) in enumerate(SIDES):
            (p0, pn), (r0, rn) = send_planes(a), send_rows(b)
            cp = pltpu.make_async_remote_copy(
                src_ref=buf.at[pl.ds(lo, count), pl.ds(p0, pn), pl.ds(r0, rn)],
                dst_ref=buf.at[pl.ds(lo, count), pl.ds(land_planes(a), pn), pl.ds(land_rows(b), rn)],
                send_sem=send.at[n], recv_sem=recv.at[n],
                device_id=neighbour(a, b, 0), device_id_type=MESH)
            cp.start()
            copies.append(cp)
        return copies

    main_copies = exchange(first, 0, 5, send_a, recv_a)
    for cp in y_copies:
        cp.wait_recv()

    def unpack_y(k, carry):
        low_lane = lax.rem(lane_v + YLOW, 64)
        from_low = lax.rem(low_lane, GROUP) < YLOW
        both = jnp.where(from_low, r_pack[1, k], r_pack[0, k])
        first[5, LOW + 2 * k, 0:BZ] = both
        first[5, LOW + 2 * k + 1, 0:BZ] = pltpu.roll(both, 64, 1)
        return carry

    lax.fori_loop(0, BX // 2, unpack_y, 0)
    halo_copies = exchange(first, 5, 1, send_b, recv_b)
    for cp in main_copies + halo_copies:
        cp.wait_recv()

    full = (2 * ROWS, BY)
    row = lax.broadcasted_iota(jnp.int32, full, 0)
    lane = lax.broadcasted_iota(jnp.int32, full, 1)
    half = row // ROWS
    zr = row - half * ROWS
    zi = gz * BZ + jnp.where(zr >= ROWS - LOW, zr - ROWS, zr)
    yi = gy * BY + jnp.where(half == 0, lane, jnp.where(lane >= BY // 2, lane - BY, lane + BY))
    in_zy = (zi >= 0) & (zi < ngz * BZ) & (yi >= 0) & (yi < ngy * BY)
    in_z1 = in_zy & (zi >= 1)
    in_y1 = in_zy & (yi >= 1)

    def x_of(j):
        return gx * BX - LOW + j

    def inside(j, comp):
        xi = x_of(j)
        high = xi < ngx * BX
        if comp == 0:
            return in_zy & ((xi >= 1) & high)
        return {1: in_z1, 2: in_y1, None: in_zy}[comp] & ((xi >= 0) & high)

    def whole(buf, count, a, j):
        packed = buf[count, j]
        halo = pltpu.roll(packed, BY - GROUP * a, 1) if a else packed
        return jnp.concatenate([buf[a, j], halo], axis=0)

    def lookup_rows(ref):
        return [jnp.full(full, ref[k], jnp.float32) for k in range(PHASES)]

    scales, powers, densities = lookup_rows(vs_ref), lookup_rows(pn_ref), lookup_rows(dn_ref)
    powers = [0.5 * (1.0 / n - 1.0) for n in powers]

    def select(phase, table):
        out = table[PHASES - 1]
        for k in range(PHASES - 2, -1, -1):
            out = jnp.where(phase == float(k), table[k], out)
        return out

    def unpack_first(j, carry):
        for a in range(3):
            vel[a, j + 1] = jnp.where(inside(j, a), whole(first, 5, a, j), 0.0)
        pres[j] = whole(first, 5, 3, j)
        phase = whole(first, 5, 4, j)
        pref[j] = jnp.where(inside(j, None), select(phase, scales), 0.0)
        expo[j] = select(phase, powers)
        rho[j] = select(phase, densities)
        return carry

    lax.fori_loop(0, PLANES, unpack_first, 0)

    def iteration(first_plane, last_plane, keep_eta):
        zero = jnp.zeros(full, jnp.float32)

        def stage(j, carry):
            eta_m, tx_m, vz_m, vy_m, fzx_m, fyx_m, pz_m, py_m, az_m, ay_m, rho_m = carry
            vx, vz, vy = vel[0, j + 1], vel[1, j + 1], vel[2, j + 1]
            rx = vel[0, j + 2] - vx
            rz = z_roll(vz, -1) - vz
            ry = y_roll(vy, -1) - vy
            div = rx + ry + rz
            third = div * (1.0 / 3.0)
            dx, dy, dz = rx - third, ry - third, rz - third
            inv = 0.5 * (dx * dx + dy * dy + dz * dz) + STRAIN_FLOOR
            eta = pref[j] * jnp.exp(expo[j] * jnp.log(inv))
            p = pres[j] - PRESSURE_STEP * eta * div
            pres[j] = p
            if keep_eta:
                eta_out[j] = eta[0:BZ]
            tx, tz, ty = eta * rx - p, eta * rz - p, eta * ry - p
            ax = eta + eta_m
            az = eta + z_roll(eta, 1)
            ay = eta + y_roll(eta, 1)
            exz = ax + z_roll(ax, 1)
            exy = ax + y_roll(ax, 1)
            eyz = ay + z_roll(ay, 1)
            fzx = exz * (vz - vz_m)
            fyx = exy * (vy - vy_m)
            fxz = exz * (vx - z_roll(vx, 1))
            fxy = exy * (vx - y_roll(vx, 1))
            fyz = eyz * (vy - z_roll(vy, 1))
            fzy = eyz * (vz - y_roll(vz, 1))
            res = tx - tx_m + 0.25 * ((z_roll(fxz, -1) - fxz) + (y_roll(fxy, -1) - fxy))
            vel[0, j + 1] = jnp.where(inside(j, 0), vx + (2.0 * VELOCITY_STEP) * res / ax, 0.0)
            res = pz_m + 0.25 * (fzx - fzx_m) - rho_m
            vel[1, j] = jnp.where(inside(j - 1, 1), vz_m + (2.0 * VELOCITY_STEP) * res / az_m, 0.0)
            res = py_m + 0.25 * (fyx - fyx_m)
            vel[2, j] = jnp.where(inside(j - 1, 2), vy_m + (2.0 * VELOCITY_STEP) * res / ay_m, 0.0)
            pz = tz - z_roll(tz, 1) + 0.25 * (y_roll(fzy, -1) - fzy)
            py = ty - y_roll(ty, 1) + 0.25 * (z_roll(fyz, -1) - fyz)
            return eta, tx, vz, vy, fzx, fyx, pz, py, az, ay, rho[j]

        lax.fori_loop(first_plane, last_plane + 1, stage, (zero,) * 11)

    iteration(0, PLANES - 2, False)
    iteration(1, PLANES - HIGH, False)

    own = lax.broadcasted_iota(jnp.int32, (BZ, BY), 1)

    def repack(i, carry):
        packed = jnp.zeros((BZ, BY), jnp.float32)
        for a in range(4):
            block = vel[a, i + LOW + 1] if a < 3 else pres[i + LOW]
            second[a, i + LOW, 0:BZ] = block[0:BZ]
            halo = block[ROWS:ROWS + BZ]
            base = GROUP * a
            if base:
                halo = pltpu.roll(halo, base, 1)
                packed = jnp.where((own >= base - YLOW) & (own < base + YHIGH), halo, packed)
            else:
                packed = halo
        second[4, i + LOW, 0:BZ] = packed
        return carry

    lax.fori_loop(0, BX, repack, 0)
    second_copies = exchange(second, 0, 5, send_c, recv_c)
    for cp in second_copies:
        cp.wait_recv()

    def unpack_second(j, carry):
        for a in range(3):
            vel[a, j + 1] = jnp.where(inside(j, a), whole(second, 4, a, j), 0.0)
        pres[j] = whole(second, 4, 3, j)
        return carry

    lax.fori_loop(0, PLANES, unpack_second, 0)
    iteration(0, PLANES - 2, False)
    iteration(1, PLANES - HIGH, True)

    total = pres[LOW, 0:BZ]
    for i in range(1, BX):
        total = total + pres[LOW + i, 0:BZ]
    base = 0
    sum_sends = []
    for n, group in enumerate(sum_phases):
        count = len(group)
        ar_src[n] = total
        for o, d in enumerate(group):
            pltpu.make_async_remote_copy(
                src_ref=ar_src.at[n], dst_ref=ar_buf.at[base + o], send_sem=ar_send.at[n], recv_sem=ar_recv.at[n],
                device_id=d, device_id_type=MESH).start()
        part = ar_buf.at[pl.ds(base, count)]
        sum_sends.append(pltpu.make_async_copy(part, part, ar_send.at[n]))
        if n == 0:
            out_ref[0] = vel[0, LOW + 1:LOW + 1 + BX, 0:BZ]
            out_ref[1] = vel[2, LOW + 1:LOW + 1 + BX, 0:BZ]
            out_ref[2] = vel[1, LOW + 1:LOW + 1 + BX, 0:BZ]
            out_ref[4] = eta_out[LOW:LOW + BX]
        pltpu.make_async_copy(part, part, ar_recv.at[n]).wait()
        for o in range(count):
            total = total + ar_buf[base + o]
        base += count
    cells = float(ngx * ngy * ngz * BX * BZ * BY)
    mean = jnp.sum(total) / cells
    out_ref[3] = pres[LOW:LOW + BX, 0:BZ] - mean

    for cp in y_copies + main_copies + halo_copies + second_copies:
        cp.wait_send()
    for cp in sum_sends:
        cp.wait()


def split_kernel(in_ref, *outs):
    for n, out in enumerate(outs):
        out[...] = in_ref[n]


def local(sizes, vel_x, vel_y, vel_z, pressure, phase, visc_scale, power_n, density):
    ngx, ngy, ngz, z_lo = sizes
    partners = (ngz - 1) + (ngx // z_lo - 1) + (z_lo * ngy - 1)
    f32 = jnp.float32
    any_spec = pl.BlockSpec(memory_space=pl.ANY)
    smem = pl.BlockSpec(memory_space=pltpu.SMEM)
    vmem = pl.BlockSpec(memory_space=pltpu.VMEM)
    dma = pltpu.SemaphoreType.DMA
    plane = (2 * ROWS, BY)
    stacked = pl.pallas_call(
        functools.partial(kernel, sizes),
        out_shape=jax.ShapeDtypeStruct((5, BX, BZ, BY), f32),
        in_specs=[any_spec] * 5 + [smem] * 3,
        out_specs=vmem,
        scratch_shapes=[
            pltpu.VMEM((BX, BZ, BY), jnp.int32),
            pltpu.VMEM((6, PLANES, ROWS, BY), f32),
            pltpu.VMEM((5, PLANES, ROWS, BY), f32),
            pltpu.VMEM((2, BX // 2, BZ, BY), f32),
            pltpu.VMEM((2, BX // 2, BZ, BY), f32),
            pltpu.VMEM((3, PLANES + 2) + plane, f32),
            pltpu.VMEM((PLANES,) + plane, f32),
            pltpu.VMEM((PLANES,) + plane, f32),
            pltpu.VMEM((PLANES,) + plane, f32),
            pltpu.VMEM((PLANES,) + plane, f32),
            pltpu.VMEM((PLANES, BZ, BY), f32),
            pltpu.VMEM((3, BZ, BY), f32),
            pltpu.VMEM((partners, BZ, BY), f32),
            dma((5,)), dma((2,)), dma((2,)),
            dma((8,)), dma((8,)), dma((8,)), dma((8,)), dma((8,)), dma((8,)),
            dma((3,)), dma((3,)),
        ],
        name="stokes",
        compiler_params=pltpu.CompilerParams(
            collective_id=0, has_side_effects=True, vmem_limit_bytes=32 * 1024 * 1024),
    )(vel_x, vel_y, vel_z, pressure, phase, visc_scale, power_n, density)
    return pl.pallas_call(
        split_kernel,
        out_shape=[jax.ShapeDtypeStruct((BX, BZ, BY), f32)] * 5,
        in_specs=[vmem],
        out_specs=[vmem] * 5,
        name="split",
    )(stacked)


def solution(mesh, z_lo=Z_LO):
    sizes = (mesh.shape["gx"], mesh.shape["gy"], mesh.shape["gz"], z_lo)
    block = P("gx", "gz", "gy")
    return jax.shard_map(
        functools.partial(local, sizes),
        mesh=mesh,
        in_specs=(block,) * 5 + (P(),) * 3,
        out_specs=(block,) * 5,
        check_vma=False,
    )
```

time: 891 us -> 96.9 us (0.11); the launches traced: 875 us -> 96.3 us
  blocking collectives: 556 us -> 0 us
  starting transfers between devices: 194 us -> 0 us
  Pallas kernels: 0 us -> 88.7 us
  other arithmetic: 63.1 us -> 0 us
  waiting for transfers between devices: 54.4 us -> 0 us
    psum x4 -> x0, blocking collectives: 556 us -> none  [pressure_sum(): return lax.psum(jnp.sum(values), ('gx', 'gy', 'gz'))]
    ppermute x48 -> x0, starting transfers between devices: 194 us -> none  [the longest x24 132 us: padded_2(): lax.ppermute(lax.slice_in_dim(block, block.shape[dim] - width, None, axis...]
    pallas_call x0 -> x2, Pallas kernels: none -> 88.7 us  [the longest x1 87 us: local(): pl.pallas_call(functools.partial(kernel, sizes), out_shape=jax.ShapeDtype...]
    ppermute x48 -> x0, waiting for transfers between devices: 54.4 us -> none  [the longest x24 47.4 us: padded_2(): lax.ppermute(lax.slice_in_dim(block, 0, width, axis=dim), axis, backward)]
    reduce_sum x4 -> x0, other arithmetic: 23.7 us -> none  [pressure_sum(): return lax.psum(jnp.sum(values), ('gx', 'gy', 'gz'))]
    another operation x13 -> x0, other arithmetic: 16.8 us -> none  [the longest x7 15.7 us: local(): jnp.stack([pressure, eta])]
    select_n x12 -> x0, other arithmetic: 15.9 us -> none  [local(): jnp.where(coord(axis_number, 0) == 0, jnp.float32(0.0), fresh)]
  transfers between devices with their start and end apart: 48 -> 0, of which waited for: 20 -> 0; matrix products, arithmetic and copies ran while one was open for 1% -> 0% of each run, Pallas kernels for 0% -> 0%
where the time goes in v1:
time: 96.9 us; the launch traced here: 96.3 us
  Pallas kernels  88.7 us (92%)
  local copies, waits for them, and re-layouts  6.87 us (7%)
    pallas_call x1, Pallas kernels, local(): pl.pallas_call(functools.partial(kernel, sizes), out_shape=jax.ShapeDtype...  87 us
    unnamed x18, local copies, waits for them, and re-layouts  6.87 us

profile of v1, /device:TPU:1, one launch (start us, length us, event | category | flops | bytes accessed | tf_op | source)
XLA Modules:
  0.0 96.3 jit_solution(205223567445723493)
XLA Ops:
  0.6 0.0 copy-start.1
  0.6 0.8 copy-done.1
  1.5 0.0 copy-start.2
  1.5 0.8 copy-done.2
  2.3 0.0 copy-start.3
  2.3 0.8 copy-done.3
  3.2 0.0 copy-start.4
  3.2 0.8 copy-done.4
  4.0 0.0 copy-start.5
  4.0 0.8 copy-done.5
  4.8 0.0 copy-start.6
  4.8 0.7 copy-done.6
  5.5 0.0 copy-start.7
  5.5 0.7 copy-done.7
  6.1 0.0 copy-start.8
  6.1 0.7 copy-done.8
  6.8 87.0 %stokes.1.in_ref = f32[5,16,8,128]{3,2,1,0:T(8,128)S(1)} custom-call(f32[16,8,128]{2,1,0:T(8,128)S(1)} %copy-done.1, f32[16,8,128]{2,1,0:T(8,128)S(1)} %copy-done.2, f32[16,8,128]{2,1,0:T(8,128)S(1)} %copy-done.3, f32[16,8,128]{2,1,0:T(8,128)S(1)} %copy-done.4, s32[16,8,128]{2,1,0:T(8,128)S(1)} %copy-done.5, f32[4]{0:T(128)S(1)} %copy-done.6, ...), custom_call_target="tpu_custom_call" | custom-call | tf_op jit(solution)/shard_map/stokes/pallas_call | solution.py:341
  93.9 0.0 copy-start
  93.9 0.7 copy-done
  94.6 1.7 %split.1 = (f32[16,8,128]{2,1,0:T(8,128)}, f32[16,8,128]{2,1,0:T(8,128)}, f32[16,8,128]{2,1,0:T(8,128)}, f32[16,8,128]{2,1,0:T(8,128)}, f32[16,8,128]{2,1,0:T(8,128)}) custom-call(f32[5,16,8,128]{3,2,1,0:T(8,128)} %copy-done), custom_call_target="tpu_custom_call" | custom-call | tf_op jit(solution)/shard_map/split/pallas_call | solution.py:368
Async XLA Ops:
  0.6 0.8 copy-start.1
  1.5 0.8 copy-start.2
  2.3 0.8 copy-start.3
  3.2 0.8 copy-start.4
  4.0 0.8 copy-start.5
  4.8 0.7 copy-start.6
  5.5 0.7 copy-start.7
  6.1 0.7 copy-start.8
  93.9 0.7 copy-start

commit v2 on v1

--- a/solution.py
+++ b/solution.py
@@ -1,4 +1,5 @@
 import functools
+import itertools
 
 import jax
 import jax.numpy as jnp
@@ -20,6 +21,7 @@
 ROWS = 2 * BZ
 GROUP = YLOW + YHIGH
 Z_LO = 4
+VMEM_BYTES = 62 * 1024 * 1024
 MESH = pl.DeviceIdType.MESH
 
 SIDES = tuple((a, b) for a in (-1, 0, 1) for b in (-1, 0, 1) if (a, b) != (0, 0))
@@ -39,6 +41,17 @@
 
 def land_rows(b):
     return {0: 0, 1: ROWS - LOW, -1: BZ}[b]
+
+
+def loop(lower, upper, body, carry, unroll):
+    assert (upper - lower) % unroll == 0
+
+    def several(n, c):
+        for u in range(unroll):
+            c = body(lower + n * unroll + u, c)
+        return c
+
+    return lax.fori_loop(0, (upper - lower) // unroll, several, carry)
 
 
 def y_roll(x, s):
@@ -54,12 +67,19 @@
     )
 
 
-def kernel(sizes, vx_ref, vy_ref, vz_ref, p_ref, ph_ref, vs_ref, pn_ref, dn_ref, out_ref,
-           ph_in, first, second, s_pack, r_pack, vel, pres, pref, expo, rho, eta_out, ar_src, ar_buf,
+def viscosity(rx, rz, ry, prefactor, power):
+    div = rx + ry + rz
+    third = div * (1.0 / 3.0)
+    dx, dy, dz = rx - third, ry - third, rz - third
+    inv = 0.5 * (dx * dx + dy * dy + dz * dz) + STRAIN_FLOOR
+    return prefactor * jnp.exp(power * jnp.log(inv)), div
+
+
+def kernel(sizes, vx_ref, vy_ref, vz_ref, p_ref, ph_ref, vs_in, pn_in, dn_in, out_ref,
+           vs_ref, pn_ref, dn_ref, ph_in, first, second, s_pack, r_pack, vel, pres, pref, expo, rho, ar_src, ar_buf,
            in_sem, ysend, yrecv, send_a, recv_a, send_b, recv_b, send_c, recv_c, ar_send, ar_recv):
     ngx, ngy, ngz, z_lo = sizes
     gx, gy, gz = lax.axis_index("gx"), lax.axis_index("gy"), lax.axis_index("gz")
-    n_x, n_z = ngx // z_lo, z_lo * ngy
 
     in_copies = []
     for n, (src, dst) in enumerate(
@@ -67,35 +87,36 @@
          (vz_ref, first.at[1, pl.ds(LOW, BX), pl.ds(0, BZ)]),
          (vy_ref, first.at[2, pl.ds(LOW, BX), pl.ds(0, BZ)]),
          (p_ref, first.at[3, pl.ds(LOW, BX), pl.ds(0, BZ)]),
-         (ph_ref, ph_in))):
+         (ph_ref, ph_in), (vs_in, vs_ref), (pn_in, pn_ref), (dn_in, dn_ref))):
         cp = pltpu.make_async_copy(src, dst, in_sem.at[n])
         cp.start()
         in_copies.append(cp)
 
+    n_x, n_y, n_z = ngx // z_lo, ngz // 2, z_lo * ngy
+
     def neighbour(a, b, c):
         return (lax.rem(gx + (a + ngx), ngx), lax.rem(gy + (c + ngy), ngy), lax.rem(gz + (b + ngz), ngz))
 
-    def along_gz(o):
-        return (gx, gy, lax.rem(gz + o, ngz))
-
-    def along_x(o):
-        return (lax.rem(gx + o * z_lo, ngx), gy, gz)
-
-    z_here = gy * z_lo + lax.rem(gx, z_lo)
-
-    def along_z(o):
-        z = lax.rem(z_here + o, n_z)
-        return (gx - lax.rem(gx, z_lo) + lax.rem(z, z_lo), z // z_lo, gz)
-
-    sum_phases = (
-        [along_gz(o) for o in range(1, ngz)],
-        [along_x(o) for o in range(1, n_x)],
-        [along_z(o) for o in range(1, n_z)],
-    )
+    chip_x, chip_y, core = gx // z_lo, gz // 2, lax.rem(gz, 2)
+    chip_z = gy * z_lo + lax.rem(gx, z_lo)
+
+    def far(x, y, z, c):
+        z = lax.rem(chip_z + z, n_z)
+        return (lax.rem(chip_x + x, n_x) * z_lo + lax.rem(z, z_lo), z // z_lo,
+                lax.rem(chip_y + y, n_y) * 2 + lax.rem(core + c, 2))
+
+    def hops(o):
+        return sum(min(d, n - d) for d, n in zip(o, (n_x, n_y, n_z, 2)))
+
+    def group(*counts):
+        offsets = [o for o in itertools.product(*[range(n) for n in counts]) if any(o)]
+        return [far(*o) for o in sorted(offsets, key=hops, reverse=True)]
+
+    sum_phases = (group(1, 1, n_z, 2), group(n_x, n_y, 1, 1))
 
     barrier = pltpu.get_barrier_semaphore()
-    greeted = [neighbour(a, b, 0) for a, b in SIDES] + [neighbour(0, 0, -1), neighbour(0, 0, 1)]
-    greeted += [d for group in sum_phases for d in group]
+    greeted = [d for devices in sum_phases for d in devices]
+    greeted += [neighbour(a, b, 0) for a, b in SIDES] + [neighbour(0, 0, -1), neighbour(0, 0, 1)]
     for d in greeted:
         pl.semaphore_signal(barrier, inc=1, device_id=d, device_id_type=MESH)
 
@@ -122,7 +143,7 @@
         s_pack[1, k] = hi
         return carry
 
-    lax.fori_loop(0, BX // 2, pack, 0)
+    loop(0, BX // 2, pack, 0, 4)
     pl.semaphore_wait(barrier, len(greeted))
 
     y_copies = []
@@ -158,7 +179,7 @@
         first[5, LOW + 2 * k + 1, 0:BZ] = pltpu.roll(both, 64, 1)
         return carry
 
-    lax.fori_loop(0, BX // 2, unpack_y, 0)
+    loop(0, BX // 2, unpack_y, 0, 8)
     halo_copies = exchange(first, 5, 1, send_b, recv_b)
     for cp in main_copies + halo_copies:
         cp.wait_recv()
@@ -211,9 +232,9 @@
         rho[j] = select(phase, densities)
         return carry
 
-    lax.fori_loop(0, PLANES, unpack_first, 0)
-
-    def iteration(first_plane, last_plane, keep_eta):
+    loop(0, PLANES, unpack_first, 0, 11)
+
+    def iteration(first_plane, last_plane):
         zero = jnp.zeros(full, jnp.float32)
 
         def stage(j, carry):
@@ -222,15 +243,9 @@
             rx = vel[0, j + 2] - vx
             rz = z_roll(vz, -1) - vz
             ry = y_roll(vy, -1) - vy
-            div = rx + ry + rz
-            third = div * (1.0 / 3.0)
-            dx, dy, dz = rx - third, ry - third, rz - third
-            inv = 0.5 * (dx * dx + dy * dy + dz * dz) + STRAIN_FLOOR
-            eta = pref[j] * jnp.exp(expo[j] * jnp.log(inv))
+            eta, div = viscosity(rx, rz, ry, pref[j], expo[j])
             p = pres[j] - PRESSURE_STEP * eta * div
             pres[j] = p
-            if keep_eta:
-                eta_out[j] = eta[0:BZ]
             tx, tz, ty = eta * rx - p, eta * rz - p, eta * ry - p
             ax = eta + eta_m
             az = eta + z_roll(eta, 1)
@@ -254,10 +269,10 @@
             py = ty - y_roll(ty, 1) + 0.25 * (z_roll(fyz, -1) - fyz)
             return eta, tx, vz, vy, fzx, fyx, pz, py, az, ay, rho[j]
 
-        lax.fori_loop(first_plane, last_plane + 1, stage, (zero,) * 11)
-
-    iteration(0, PLANES - 2, False)
-    iteration(1, PLANES - HIGH, False)
+        loop(first_plane, last_plane + 1, stage, (zero,) * 11, (last_plane + 1 - first_plane) // 3)
+
+    iteration(0, PLANES - 2)
+    iteration(1, PLANES - HIGH)
 
     own = lax.broadcasted_iota(jnp.int32, (BZ, BY), 1)
 
@@ -276,7 +291,7 @@
         second[4, i + LOW, 0:BZ] = packed
         return carry
 
-    lax.fori_loop(0, BX, repack, 0)
+    loop(0, BX, repack, 0, 8)
     second_copies = exchange(second, 0, 5, send_c, recv_c)
     for cp in second_copies:
         cp.wait_recv()
@@ -287,36 +302,51 @@
         pres[j] = whole(second, 4, 3, j)
         return carry
 
-    lax.fori_loop(0, PLANES, unpack_second, 0)
-    iteration(0, PLANES - 2, False)
-    iteration(1, PLANES - HIGH, True)
-
-    total = pres[LOW, 0:BZ]
-    for i in range(1, BX):
-        total = total + pres[LOW + i, 0:BZ]
+    loop(0, PLANES, unpack_second, 0, 11)
+    iteration(0, PLANES - 2)
+
+    lane_0 = lane_v == 0
+
+    def last_pressure(i, total):
+        j = i + LOW
+        vx = vel[0, j + 1, 0:BZ]
+        vz = vel[1, j + 1, 0:ROWS]
+        vy = vel[2, j + 1, 0:BZ]
+        rx = vel[0, j + 2, 0:BZ] - vx
+        rz = (pltpu.roll(vz, ROWS - 1, 0) - vz)[0:BZ]
+        next_y = jnp.where(lane_0, vel[2, j + 1, ROWS:ROWS + BZ], vy)
+        ry = pltpu.roll(next_y, BY - 1, 1) - vy
+        eta, div = viscosity(rx, rz, ry, pref[j, 0:BZ], expo[j, 0:BZ])
+        p = pres[j, 0:BZ] - PRESSURE_STEP * eta * div
+        out_ref[3, i] = p
+        out_ref[4, i] = eta
+        return total + p
+
+    total = loop(0, BX, last_pressure, jnp.zeros((BZ, BY), jnp.float32), 8)
+
     base = 0
     sum_sends = []
-    for n, group in enumerate(sum_phases):
-        count = len(group)
+    for n, devices in enumerate(sum_phases):
+        count = len(devices)
         ar_src[n] = total
-        for o, d in enumerate(group):
+        for o, d in enumerate(devices):
             pltpu.make_async_remote_copy(
                 src_ref=ar_src.at[n], dst_ref=ar_buf.at[base + o], send_sem=ar_send.at[n], recv_sem=ar_recv.at[n],
                 device_id=d, device_id_type=MESH).start()
         part = ar_buf.at[pl.ds(base, count)]
         sum_sends.append(pltpu.make_async_copy(part, part, ar_send.at[n]))
         if n == 0:
+            iteration(1, PLANES - HIGH)
             out_ref[0] = vel[0, LOW + 1:LOW + 1 + BX, 0:BZ]
             out_ref[1] = vel[2, LOW + 1:LOW + 1 + BX, 0:BZ]
             out_ref[2] = vel[1, LOW + 1:LOW + 1 + BX, 0:BZ]
-            out_ref[4] = eta_out[LOW:LOW + BX]
         pltpu.make_async_copy(part, part, ar_recv.at[n]).wait()
         for o in range(count):
             total = total + ar_buf[base + o]
         base += count
     cells = float(ngx * ngy * ngz * BX * BZ * BY)
     mean = jnp.sum(total) / cells
-    out_ref[3] = pres[LOW:LOW + BX, 0:BZ] - mean
+    out_ref[3] = out_ref[3] - mean
 
     for cp in y_copies + main_copies + halo_copies + second_copies:
         cp.wait_send()
@@ -324,26 +354,32 @@
         cp.wait()
 
 
-def split_kernel(in_ref, *outs):
-    for n, out in enumerate(outs):
-        out[...] = in_ref[n]
+def split_kernel(in_ref, *refs):
+    *outs, sem = refs
+    copies = [pltpu.make_async_copy(in_ref.at[n], out, sem.at[n]) for n, out in enumerate(outs)]
+    for cp in copies:
+        cp.start()
+    for cp in copies:
+        cp.wait()
 
 
 def local(sizes, vel_x, vel_y, vel_z, pressure, phase, visc_scale, power_n, density):
     ngx, ngy, ngz, z_lo = sizes
-    partners = (ngz - 1) + (ngx // z_lo - 1) + (z_lo * ngy - 1)
+    partners = (z_lo * ngy * 2 - 1) + (ngx // z_lo * (ngz // 2) - 1)
     f32 = jnp.float32
-    any_spec = pl.BlockSpec(memory_space=pl.ANY)
-    smem = pl.BlockSpec(memory_space=pltpu.SMEM)
+    hbm = pl.BlockSpec(memory_space=pltpu.HBM)
     vmem = pl.BlockSpec(memory_space=pltpu.VMEM)
     dma = pltpu.SemaphoreType.DMA
     plane = (2 * ROWS, BY)
     stacked = pl.pallas_call(
         functools.partial(kernel, sizes),
         out_shape=jax.ShapeDtypeStruct((5, BX, BZ, BY), f32),
-        in_specs=[any_spec] * 5 + [smem] * 3,
+        in_specs=[hbm] * 8,
         out_specs=vmem,
         scratch_shapes=[
+            pltpu.SMEM((PHASES,), f32),
+            pltpu.SMEM((PHASES,), f32),
+            pltpu.SMEM((PHASES,), f32),
             pltpu.VMEM((BX, BZ, BY), jnp.int32),
             pltpu.VMEM((6, PLANES, ROWS, BY), f32),
             pltpu.VMEM((5, PLANES, ROWS, BY), f32),
@@ -354,23 +390,24 @@
             pltpu.VMEM((PLANES,) + plane, f32),
             pltpu.VMEM((PLANES,) + plane, f32),
             pltpu.VMEM((PLANES,) + plane, f32),
-            pltpu.VMEM((PLANES, BZ, BY), f32),
-            pltpu.VMEM((3, BZ, BY), f32),
+            pltpu.VMEM((2, BZ, BY), f32),
             pltpu.VMEM((partners, BZ, BY), f32),
-            dma((5,)), dma((2,)), dma((2,)),
+            dma((8,)), dma((2,)), dma((2,)),
             dma((8,)), dma((8,)), dma((8,)), dma((8,)), dma((8,)), dma((8,)),
-            dma((3,)), dma((3,)),
+            dma((2,)), dma((2,)),
         ],
         name="stokes",
         compiler_params=pltpu.CompilerParams(
-            collective_id=0, has_side_effects=True, vmem_limit_bytes=32 * 1024 * 1024),
+            collective_id=0, has_side_effects=True, vmem_limit_bytes=VMEM_BYTES),
     )(vel_x, vel_y, vel_z, pressure, phase, visc_scale, power_n, density)
     return pl.pallas_call(
         split_kernel,
         out_shape=[jax.ShapeDtypeStruct((BX, BZ, BY), f32)] * 5,
-        in_specs=[vmem],
-        out_specs=[vmem] * 5,
+        in_specs=[hbm],
+        out_specs=[hbm] * 5,
+        scratch_shapes=[dma((5,))],
         name="split",
+        compiler_params=pltpu.CompilerParams(vmem_limit_bytes=VMEM_BYTES),
     )(stacked)
 
 

time: 96.9 us -> 78.2 us (0.81)
  Pallas kernels: 88.7 us -> 77.3 us
  local copies, waits for them, and re-layouts: 6.87 us -> 0 us
    pallas_call x1, Pallas kernels: 87 us -> 66.2 us  [local(): pl.pallas_call(functools.partial(kernel, sizes), out_shape=jax.ShapeDtype...]
    pallas_call x1, Pallas kernels: 1.69 us -> 11.1 us  [local(): pl.pallas_call(split_kernel, out_shape=[jax.ShapeDtypeStruct((BX, BZ, BY)...]
    unnamed x18 -> x0, local copies, waits for them, and re-layouts: 6.87 us -> none
where the time goes in v2:
time: 78.2 us; the launch traced here: 78 us
  Pallas kernels  77.3 us (99%)
    pallas_call x1, Pallas kernels, local(): pl.pallas_call(functools.partial(kernel, sizes), out_shape=jax.ShapeDtype...  66.2 us
    pallas_call x1, Pallas kernels, local(): pl.pallas_call(split_kernel, out_shape=[jax.ShapeDtypeStruct((BX, BZ, BY)...  11.1 us

profile of v2, /device:TPU:1, one launch (start us, length us, event | category | flops | bytes accessed | tf_op | source)
XLA Modules:
  0.0 78.0 jit_solution(910991778489684022)
XLA Ops:
  0.6 66.2 %stokes.1.in_ref = f32[5,16,8,128]{3,2,1,0:T(8,128)} custom-call(f32[16,8,128]{2,1,0:T(8,128)} %vx_ref.1, f32[16,8,128]{2,1,0:T(8,128)} %vy_ref.1, f32[16,8,128]{2,1,0:T(8,128)} %vz_ref.1, f32[16,8,128]{2,1,0:T(8,128)} %p_ref.1, s32[16,8,128]{2,1,0:T(8,128)} %ph_ref.1, f32[4]{0:T(128)} %vs_in.1, f32[4]{0:T(128)} %pn_in.1, f32[4]{0:T(128)} %dn_in.1), custom_call_target="tpu_custom_call" | custom-call | tf_op jit(solution)/shard_map/stokes/pallas_call | solution.py:374
  66.9 11.1 %split.1 = (f32[16,8,128]{2,1,0:T(8,128)}, f32[16,8,128]{2,1,0:T(8,128)}, f32[16,8,128]{2,1,0:T(8,128)}, f32[16,8,128]{2,1,0:T(8,128)}, f32[16,8,128]{2,1,0:T(8,128)}) custom-call(f32[5,16,8,128]{3,2,1,0:T(8,128)} %stokes.1.in_ref), custom_call_target="tpu_custom_call" | custom-call | tf_op jit(solution)/shard_map/split/pallas_call | solution.py:403

commit v3 on v2

--- a/solution.py
+++ b/solution.py
@@ -76,8 +76,8 @@
 
 
 def kernel(sizes, vx_ref, vy_ref, vz_ref, p_ref, ph_ref, vs_in, pn_in, dn_in, out_ref,
-           vs_ref, pn_ref, dn_ref, ph_in, first, second, s_pack, r_pack, vel, pres, pref, expo, rho, ar_src, ar_buf,
-           in_sem, ysend, yrecv, send_a, recv_a, send_b, recv_b, send_c, recv_c, ar_send, ar_recv):
+           vs_ref, pn_ref, dn_ref, ph_in, first, second, s_pack, r_pack, vel, pres, pref, expo, rho, last_p, last_eta, ar_src, ar_buf,
+           in_sem, ysend, yrecv, send_a, recv_a, send_b, recv_b, send_c, recv_c, ar_send, ar_recv, out_sem, here):
     ngx, ngy, ngz, z_lo = sizes
     gx, gy, gz = lax.axis_index("gx"), lax.axis_index("gy"), lax.axis_index("gz")
 
@@ -115,8 +115,7 @@
     sum_phases = (group(1, 1, n_z, 2), group(n_x, n_y, 1, 1))
 
     barrier = pltpu.get_barrier_semaphore()
-    greeted = [d for devices in sum_phases for d in devices]
-    greeted += [neighbour(a, b, 0) for a, b in SIDES] + [neighbour(0, 0, -1), neighbour(0, 0, 1)]
+    greeted = [neighbour(0, 0, -1), neighbour(0, 0, 1)] + [neighbour(a, b, 0) for a, b in SIDES]
     for d in greeted:
         pl.semaphore_signal(barrier, inc=1, device_id=d, device_id_type=MESH)
 
@@ -293,6 +292,8 @@
 
     loop(0, BX, repack, 0, 8)
     second_copies = exchange(second, 0, 5, send_c, recv_c)
+    for a, b in SIDES:
+        pl.semaphore_signal(here.at[0], inc=1, device_id=neighbour(2 * a, 2 * b, 0), device_id_type=MESH)
     for cp in second_copies:
         cp.wait_recv()
 
@@ -318,17 +319,22 @@
         ry = pltpu.roll(next_y, BY - 1, 1) - vy
         eta, div = viscosity(rx, rz, ry, pref[j, 0:BZ], expo[j, 0:BZ])
         p = pres[j, 0:BZ] - PRESSURE_STEP * eta * div
-        out_ref[3, i] = p
-        out_ref[4, i] = eta
+        last_p[i] = p
+        last_eta[i] = eta
         return total + p
 
     total = loop(0, BX, last_pressure, jnp.zeros((BZ, BY), jnp.float32), 8)
 
+    total = jnp.sum(total, axis=0, keepdims=True)
+    eta_copy = pltpu.make_async_copy(last_eta, out_ref.at[4], out_sem.at[4])
+    eta_copy.start()
+    out_copies = [eta_copy]
     base = 0
     sum_sends = []
     for n, devices in enumerate(sum_phases):
         count = len(devices)
         ar_src[n] = total
+        pl.semaphore_wait(here.at[n], len(SIDES))
         for o, d in enumerate(devices):
             pltpu.make_async_remote_copy(
                 src_ref=ar_src.at[n], dst_ref=ar_buf.at[base + o], send_sem=ar_send.at[n], recv_sem=ar_recv.at[n],
@@ -336,30 +342,41 @@
         part = ar_buf.at[pl.ds(base, count)]
         sum_sends.append(pltpu.make_async_copy(part, part, ar_send.at[n]))
         if n == 0:
+            for a, b in SIDES:
+                pl.semaphore_signal(here.at[1], inc=1, device_id=neighbour(4 * a, 4 * b, 0), device_id_type=MESH)
             iteration(1, PLANES - HIGH)
-            out_ref[0] = vel[0, LOW + 1:LOW + 1 + BX, 0:BZ]
-            out_ref[1] = vel[2, LOW + 1:LOW + 1 + BX, 0:BZ]
-            out_ref[2] = vel[1, LOW + 1:LOW + 1 + BX, 0:BZ]
+            for a, comp in enumerate((0, 2, 1)):
+                out_v = vel.at[comp, pl.ds(LOW + 1, BX), pl.ds(0, BZ)]
+                cp = pltpu.make_async_copy(out_v, out_ref.at[a], out_sem.at[a])
+                cp.start()
+                out_copies.append(cp)
         pltpu.make_async_copy(part, part, ar_recv.at[n]).wait()
         for o in range(count):
             total = total + ar_buf[base + o]
         base += count
     cells = float(ngx * ngy * ngz * BX * BZ * BY)
     mean = jnp.sum(total) / cells
-    out_ref[3] = out_ref[3] - mean
+    last_p[...] = last_p[...] - mean
+    p_copy = pltpu.make_async_copy(last_p, out_ref.at[3], out_sem.at[3])
+    p_copy.start()
+    out_copies.append(p_copy)
 
     for cp in y_copies + main_copies + halo_copies + second_copies:
         cp.wait_send()
-    for cp in sum_sends:
+    for cp in sum_sends + out_copies:
         cp.wait()
 
 
 def split_kernel(in_ref, *refs):
-    *outs, sem = refs
-    copies = [pltpu.make_async_copy(in_ref.at[n], out, sem.at[n]) for n, out in enumerate(outs)]
-    for cp in copies:
+    *outs, held, sem_in, sem_out = refs
+    into = [pltpu.make_async_copy(in_ref.at[n], held.at[n], sem_in.at[n]) for n in range(5)]
+    back = [pltpu.make_async_copy(held.at[n], out, sem_out.at[n]) for n, out in enumerate(outs)]
+    for cp in into:
         cp.start()
-    for cp in copies:
+    for cp, after in zip(into, back):
+        cp.wait()
+        after.start()
+    for cp in back:
         cp.wait()
 
 
@@ -368,14 +385,13 @@
     partners = (z_lo * ngy * 2 - 1) + (ngx // z_lo * (ngz // 2) - 1)
     f32 = jnp.float32
     hbm = pl.BlockSpec(memory_space=pltpu.HBM)
-    vmem = pl.BlockSpec(memory_space=pltpu.VMEM)
     dma = pltpu.SemaphoreType.DMA
     plane = (2 * ROWS, BY)
     stacked = pl.pallas_call(
         functools.partial(kernel, sizes),
         out_shape=jax.ShapeDtypeStruct((5, BX, BZ, BY), f32),
         in_specs=[hbm] * 8,
-        out_specs=vmem,
+        out_specs=hbm,
         scratch_shapes=[
             pltpu.SMEM((PHASES,), f32),
             pltpu.SMEM((PHASES,), f32),
@@ -390,11 +406,13 @@
             pltpu.VMEM((PLANES,) + plane, f32),
             pltpu.VMEM((PLANES,) + plane, f32),
             pltpu.VMEM((PLANES,) + plane, f32),
-            pltpu.VMEM((2, BZ, BY), f32),
-            pltpu.VMEM((partners, BZ, BY), f32),
+            pltpu.VMEM((BX, BZ, BY), f32),
+            pltpu.VMEM((BX, BZ, BY), f32),
+            pltpu.VMEM((2, 1, BY), f32),
+            pltpu.VMEM((partners, 1, BY), f32),
             dma((8,)), dma((2,)), dma((2,)),
             dma((8,)), dma((8,)), dma((8,)), dma((8,)), dma((8,)), dma((8,)),
-            dma((2,)), dma((2,)),
+            dma((2,)), dma((2,)), dma((5,)), pltpu.SemaphoreType.REGULAR((2,)),
         ],
         name="stokes",
         compiler_params=pltpu.CompilerParams(
@@ -405,7 +423,7 @@
         out_shape=[jax.ShapeDtypeStruct((BX, BZ, BY), f32)] * 5,
         in_specs=[hbm],
         out_specs=[hbm] * 5,
-        scratch_shapes=[dma((5,))],
+        scratch_shapes=[pltpu.VMEM((5, BX, BZ, BY), f32), dma((5,)), dma((5,))],
         name="split",
         compiler_params=pltpu.CompilerParams(vmem_limit_bytes=VMEM_BYTES),
     )(stacked)

time: 78.2 us -> 63.7 us (0.81)
  Pallas kernels: 77.3 us -> 62.8 us
    pallas_call x1, Pallas kernels: 11.1 us -> 1.68 us  [local(): pl.pallas_call(split_kernel, out_shape=[jax.ShapeDtypeStruct((BX, BZ, BY)...]
    pallas_call x1, Pallas kernels: 66.2 us -> 61.1 us  [local(): pl.pallas_call(functools.partial(kernel, sizes), out_shape=jax.ShapeDtype...]
where the time goes in v3:
time: 63.7 us; the launch traced here: 63.5 us
  Pallas kernels  62.8 us (99%)
  between operations  0.64 us (1%)
    pallas_call x1, Pallas kernels, local(): pl.pallas_call(functools.partial(kernel, sizes), out_shape=jax.ShapeDtype...  61.1 us
    pallas_call x1, Pallas kernels, local(): pl.pallas_call(split_kernel, out_shape=[jax.ShapeDtypeStruct((BX, BZ, BY)...  1.68 us

profile of v3, /device:TPU:1, one launch (start us, length us, event | category | flops | bytes accessed | tf_op | source)
XLA Modules:
  0.0 63.5 jit_solution(13498161538306588692)
XLA Ops:
  0.6 61.1 %stokes.1.in_ref = f32[5,16,8,128]{3,2,1,0:T(8,128)} custom-call(f32[16,8,128]{2,1,0:T(8,128)} %vx_ref.1, f32[16,8,128]{2,1,0:T(8,128)} %vy_ref.1, f32[16,8,128]{2,1,0:T(8,128)} %vz_ref.1, f32[16,8,128]{2,1,0:T(8,128)} %p_ref.1, s32[16,8,128]{2,1,0:T(8,128)} %ph_ref.1, f32[4]{0:T(128)} %vs_in.1, f32[4]{0:T(128)} %pn_in.1, f32[4]{0:T(128)} %dn_in.1), custom_call_target="tpu_custom_call" | custom-call | tf_op jit(solution)/shard_map/stokes/pallas_call | solution.py:390
  61.8 1.7 %split.1 = (f32[16,8,128]{2,1,0:T(8,128)}, f32[16,8,128]{2,1,0:T(8,128)}, f32[16,8,128]{2,1,0:T(8,128)}, f32[16,8,128]{2,1,0:T(8,128)}, f32[16,8,128]{2,1,0:T(8,128)}) custom-call(f32[5,16,8,128]{3,2,1,0:T(8,128)} %stokes.1.in_ref), custom_call_target="tpu_custom_call" | custom-call | tf_op jit(solution)/shard_map/split/pallas_call | solution.py:421

commit v4 on v3

--- a/solution.py
+++ b/solution.py
@@ -20,6 +20,8 @@
 PLANES = BX + LOW + HIGH
 ROWS = 2 * BZ
 GROUP = YLOW + YHIGH
+SHIFT = YHIGH + YLOW
+LEFT_AT, LEFT = 118, 30
 Z_LO = 4
 VMEM_BYTES = 62 * 1024 * 1024
 MESH = pl.DeviceIdType.MESH
@@ -55,16 +57,11 @@
 
 
 def y_roll(x, s):
-    r = pltpu.roll(x, s % BY, 1)
-    swapped = jnp.concatenate([r[ROWS:], r[:ROWS]], axis=0)
-    lane = lax.broadcasted_iota(jnp.int32, x.shape, 1)
-    return jnp.where(lane == (0 if s == 1 else BY - 1), swapped, r)
+    return pltpu.roll(x, s % BY, 1)
 
 
 def z_roll(x, s):
-    return jnp.concatenate(
-        [pltpu.roll(x[:ROWS], s % ROWS, 0), pltpu.roll(x[ROWS:], s % ROWS, 0)], axis=0
-    )
+    return pltpu.roll(x, s % ROWS, 0)
 
 
 def viscosity(rx, rz, ry, prefactor, power):
@@ -76,10 +73,37 @@
 
 
 def kernel(sizes, vx_ref, vy_ref, vz_ref, p_ref, ph_ref, vs_in, pn_in, dn_in, out_ref,
-           vs_ref, pn_ref, dn_ref, ph_in, first, second, s_pack, r_pack, vel, pres, pref, expo, rho, last_p, last_eta, ar_src, ar_buf,
-           in_sem, ysend, yrecv, send_a, recv_a, send_b, recv_b, send_c, recv_c, ar_send, ar_recv, out_sem, here):
+           vs_ref, pn_ref, dn_ref, ph_in, first, second, s_pack, r_pack, vel, pres, pref, expo, rho, last_v, last_p, last_eta, ar_src, ar_buf,
+           in_sem, ysend, yrecv, send_a, recv_a, send_b, recv_b, send_c, recv_c, send_d, recv_d, ar_send, ar_recv, out_sem, here):
     ngx, ngy, ngz, z_lo = sizes
     gx, gy, gz = lax.axis_index("gx"), lax.axis_index("gy"), lax.axis_index("gz")
+
+    n_x, n_y, n_z = ngx // z_lo, ngz // 2, z_lo * ngy
+
+    def neighbour(a, b, c):
+        return (lax.rem(gx + (a + ngx), ngx), lax.rem(gy + (c + ngy), ngy), lax.rem(gz + (b + ngz), ngz))
+
+    chip_x, chip_y, core = gx // z_lo, gz // 2, lax.rem(gz, 2)
+    chip_z = gy * z_lo + lax.rem(gx, z_lo)
+
+    def far(x, y, z, c):
+        z = lax.rem(chip_z + z, n_z)
+        return (lax.rem(chip_x + x, n_x) * z_lo + lax.rem(z, z_lo), z // z_lo,
+                lax.rem(chip_y + y, n_y) * 2 + lax.rem(core + c, 2))
+
+    def hops(o):
+        return sum(min(d, n - d) for d, n in zip(o, (n_x, n_y, n_z, 2)))
+
+    def group(*counts):
+        offsets = [o for o in itertools.product(*[range(n) for n in counts]) if any(o)]
+        return [far(*o) for o in sorted(offsets, key=hops, reverse=True)]
+
+    sum_phases = (group(1, 1, n_z, 2), group(n_x, n_y, 1, 1))
+
+    barrier = pltpu.get_barrier_semaphore()
+    greeted = [neighbour(0, 0, -1), neighbour(0, 0, 1)] + [neighbour(a, b, 0) for a, b in SIDES]
+    for d in greeted:
+        pl.semaphore_signal(barrier, inc=1, device_id=d, device_id_type=MESH)
 
     in_copies = []
     for n, (src, dst) in enumerate(
@@ -92,32 +116,6 @@
         cp.start()
         in_copies.append(cp)
 
-    n_x, n_y, n_z = ngx // z_lo, ngz // 2, z_lo * ngy
-
-    def neighbour(a, b, c):
-        return (lax.rem(gx + (a + ngx), ngx), lax.rem(gy + (c + ngy), ngy), lax.rem(gz + (b + ngz), ngz))
-
-    chip_x, chip_y, core = gx // z_lo, gz // 2, lax.rem(gz, 2)
-    chip_z = gy * z_lo + lax.rem(gx, z_lo)
-
-    def far(x, y, z, c):
-        z = lax.rem(chip_z + z, n_z)
-        return (lax.rem(chip_x + x, n_x) * z_lo + lax.rem(z, z_lo), z // z_lo,
-                lax.rem(chip_y + y, n_y) * 2 + lax.rem(core + c, 2))
-
-    def hops(o):
-        return sum(min(d, n - d) for d, n in zip(o, (n_x, n_y, n_z, 2)))
-
-    def group(*counts):
-        offsets = [o for o in itertools.product(*[range(n) for n in counts]) if any(o)]
-        return [far(*o) for o in sorted(offsets, key=hops, reverse=True)]
-
-    sum_phases = (group(1, 1, n_z, 2), group(n_x, n_y, 1, 1))
-
-    barrier = pltpu.get_barrier_semaphore()
-    greeted = [neighbour(0, 0, -1), neighbour(0, 0, 1)] + [neighbour(a, b, 0) for a, b in SIDES]
-    for d in greeted:
-        pl.semaphore_signal(barrier, inc=1, device_id=d, device_id_type=MESH)
 
     lane_v = lax.broadcasted_iota(jnp.int32, (BZ, BY), 1)
     for cp in in_copies:
@@ -180,39 +178,27 @@
 
     loop(0, BX // 2, unpack_y, 0, 8)
     halo_copies = exchange(first, 5, 1, send_b, recv_b)
-    for cp in main_copies + halo_copies:
-        cp.wait_recv()
-
-    full = (2 * ROWS, BY)
+
+    full = (ROWS, BY)
     row = lax.broadcasted_iota(jnp.int32, full, 0)
     lane = lax.broadcasted_iota(jnp.int32, full, 1)
-    half = row // ROWS
-    zr = row - half * ROWS
-    zi = gz * BZ + jnp.where(zr >= ROWS - LOW, zr - ROWS, zr)
-    yi = gy * BY + jnp.where(half == 0, lane, jnp.where(lane >= BY // 2, lane - BY, lane + BY))
-    in_zy = (zi >= 0) & (zi < ngz * BZ) & (yi >= 0) & (yi < ngy * BY)
-    in_z1 = in_zy & (zi >= 1)
-    in_y1 = in_zy & (yi >= 1)
-
-    def x_of(j):
-        return gx * BX - LOW + j
-
-    def inside(j, comp):
-        xi = x_of(j)
-        high = xi < ngx * BX
-        if comp == 0:
-            return in_zy & ((xi >= 1) & high)
-        return {1: in_z1, 2: in_y1, None: in_zy}[comp] & ((xi >= 0) & high)
-
-    def whole(buf, count, a, j):
-        packed = buf[count, j]
-        halo = pltpu.roll(packed, BY - GROUP * a, 1) if a else packed
-        return jnp.concatenate([buf[a, j], halo], axis=0)
-
-    def lookup_rows(ref):
+    zi = gz * BZ + jnp.where(row >= ROWS - LOW, row - ROWS, row)
+    in_strip = jnp.where(lane < YHIGH, lane + BY, jnp.where(lane < BY // 2, lane - SHIFT, lane))
+    in_z = (zi >= 0) & (zi < ngz * BZ)
+    masks = []
+    for cell in (lane, in_strip):
+        yi = gy * BY + cell
+        in_zy = in_z & (yi >= 0) & (yi < ngy * BY)
+        masks.append({None: in_zy, 0: in_zy, 1: in_zy & (zi >= 1), 2: in_zy & (yi >= 1)})
+
+    def inside(part, j, comp):
+        xi = gx * BX - LOW + j
+        return masks[part][comp] & ((xi >= (1 if comp == 0 else 0)) & (xi < ngx * BX))
+
+    def splat(ref):
         return [jnp.full(full, ref[k], jnp.float32) for k in range(PHASES)]
 
-    scales, powers, densities = lookup_rows(vs_ref), lookup_rows(pn_ref), lookup_rows(dn_ref)
+    scales, powers, densities = splat(vs_ref), splat(pn_ref), splat(dn_ref)
     powers = [0.5 * (1.0 / n - 1.0) for n in powers]
 
     def select(phase, table):
@@ -221,30 +207,51 @@
             out = jnp.where(phase == float(k), table[k], out)
         return out
 
-    def unpack_first(j, carry):
+    def unpack_first(part, j, whole):
         for a in range(3):
-            vel[a, j + 1] = jnp.where(inside(j, a), whole(first, 5, a, j), 0.0)
-        pres[j] = whole(first, 5, 3, j)
-        phase = whole(first, 5, 4, j)
-        pref[j] = jnp.where(inside(j, None), select(phase, scales), 0.0)
-        expo[j] = select(phase, powers)
-        rho[j] = select(phase, densities)
-        return carry
-
-    loop(0, PLANES, unpack_first, 0, 11)
-
-    def iteration(first_plane, last_plane):
+            vel[part, a, j + 1] = jnp.where(inside(part, j, a), whole(a, j), 0.0)
+        pres[part, j] = whole(3, j)
+        phase = whole(4, j)
+        pref[part, j] = jnp.where(inside(part, j, None), select(phase, scales), 0.0)
+        expo[part, j] = select(phase, powers)
+        rho[part, j] = select(phase, densities)
+
+    def unpack_second(part, j, whole):
+        for a in range(3):
+            vel[part, a, j + 1] = jnp.where(inside(part, j, a), whole(a, j), 0.0)
+        pres[part, j] = whole(3, j)
+
+    def strip_first(a, j):
+        main = first[a, j]
+        halo = first[5, j]
+        if a:
+            halo = pltpu.roll(halo, BY - GROUP * a, 1)
+        low = pltpu.roll(jnp.where(lane >= BY - YLOW, halo, main), SHIFT, 1)
+        return jnp.where(lane < YHIGH, halo, jnp.where(lane < BY // 2, low, main))
+
+    def strip_second(a, j):
+        packed = second[4, j]
+        return pltpu.roll(packed, BY - LEFT * a, 1) if a else packed
+
+    def unpack(function, part, whole):
+        def body(j, carry):
+            function(part, j, whole)
+            return carry
+
+        loop(0, PLANES, body, 0, 11)
+
+    def iteration(part, first_plane, last_plane):
         zero = jnp.zeros(full, jnp.float32)
 
         def stage(j, carry):
             eta_m, tx_m, vz_m, vy_m, fzx_m, fyx_m, pz_m, py_m, az_m, ay_m, rho_m = carry
-            vx, vz, vy = vel[0, j + 1], vel[1, j + 1], vel[2, j + 1]
-            rx = vel[0, j + 2] - vx
+            vx, vz, vy = vel[part, 0, j + 1], vel[part, 1, j + 1], vel[part, 2, j + 1]
+            rx = vel[part, 0, j + 2] - vx
             rz = z_roll(vz, -1) - vz
             ry = y_roll(vy, -1) - vy
-            eta, div = viscosity(rx, rz, ry, pref[j], expo[j])
-            p = pres[j] - PRESSURE_STEP * eta * div
-            pres[j] = p
+            eta, div = viscosity(rx, rz, ry, pref[part, j], expo[part, j])
+            p = pres[part, j] - PRESSURE_STEP * eta * div
+            pres[part, j] = p
             tx, tz, ty = eta * rx - p, eta * rz - p, eta * ry - p
             ax = eta + eta_m
             az = eta + z_roll(eta, 1)
@@ -259,66 +266,85 @@
             fyz = eyz * (vy - z_roll(vy, 1))
             fzy = eyz * (vz - y_roll(vz, 1))
             res = tx - tx_m + 0.25 * ((z_roll(fxz, -1) - fxz) + (y_roll(fxy, -1) - fxy))
-            vel[0, j + 1] = jnp.where(inside(j, 0), vx + (2.0 * VELOCITY_STEP) * res / ax, 0.0)
+            vel[part, 0, j + 1] = jnp.where(inside(part, j, 0), vx + (2.0 * VELOCITY_STEP) * res / ax, 0.0)
             res = pz_m + 0.25 * (fzx - fzx_m) - rho_m
-            vel[1, j] = jnp.where(inside(j - 1, 1), vz_m + (2.0 * VELOCITY_STEP) * res / az_m, 0.0)
+            vel[part, 1, j] = jnp.where(inside(part, j - 1, 1), vz_m + (2.0 * VELOCITY_STEP) * res / az_m, 0.0)
             res = py_m + 0.25 * (fyx - fyx_m)
-            vel[2, j] = jnp.where(inside(j - 1, 2), vy_m + (2.0 * VELOCITY_STEP) * res / ay_m, 0.0)
+            vel[part, 2, j] = jnp.where(inside(part, j - 1, 2), vy_m + (2.0 * VELOCITY_STEP) * res / ay_m, 0.0)
             pz = tz - z_roll(tz, 1) + 0.25 * (y_roll(fzy, -1) - fzy)
             py = ty - y_roll(ty, 1) + 0.25 * (z_roll(fyz, -1) - fyz)
-            return eta, tx, vz, vy, fzx, fyx, pz, py, az, ay, rho[j]
+            return eta, tx, vz, vy, fzx, fyx, pz, py, az, ay, rho[part, j]
 
         loop(first_plane, last_plane + 1, stage, (zero,) * 11, (last_plane + 1 - first_plane) // 3)
 
-    iteration(0, PLANES - 2)
-    iteration(1, PLANES - HIGH)
-
-    own = lax.broadcasted_iota(jnp.int32, (BZ, BY), 1)
-
-    def repack(i, carry):
-        packed = jnp.zeros((BZ, BY), jnp.float32)
+    def odd(part):
+        iteration(part, 0, PLANES - 2)
+
+    def even(part):
+        iteration(part, 1, PLANES - HIGH)
+
+    def field(part, a, i):
+        return vel[part, a, i + LOW + 1, 0:BZ] if a < 3 else pres[part, i + LOW, 0:BZ]
+
+    for cp in main_copies:
+        cp.wait_recv()
+    unpack(unpack_first, 0, lambda a, j: first[a, j])
+    odd(0)
+    even(0)
+
+    def repack_main(i, carry):
         for a in range(4):
-            block = vel[a, i + LOW + 1] if a < 3 else pres[i + LOW]
-            second[a, i + LOW, 0:BZ] = block[0:BZ]
-            halo = block[ROWS:ROWS + BZ]
-            base = GROUP * a
-            if base:
-                halo = pltpu.roll(halo, base, 1)
-                packed = jnp.where((own >= base - YLOW) & (own < base + YHIGH), halo, packed)
-            else:
-                packed = halo
+            second[a, i + LOW, 0:BZ] = field(0, a, i)
+        return carry
+
+    loop(0, BX, repack_main, 0, 8)
+    main_second = exchange(second, 0, 4, send_c, recv_c)
+
+    for cp in halo_copies:
+        cp.wait_recv()
+    unpack(unpack_first, 1, strip_first)
+    odd(1)
+    even(1)
+
+    def repack_strip(i, carry):
+        packed = field(1, 0, i)
+        place = lane_v + jnp.where(lane_v >= LEFT_AT, -LEFT_AT, BY - LEFT_AT)
+        for a in range(1, 4):
+            rolled = pltpu.roll(field(1, a, i), LEFT * a, 1)
+            packed = jnp.where((place >= LEFT * a) & (place < LEFT * (a + 1)), rolled, packed)
         second[4, i + LOW, 0:BZ] = packed
         return carry
 
-    loop(0, BX, repack, 0, 8)
-    second_copies = exchange(second, 0, 5, send_c, recv_c)
+    loop(0, BX, repack_strip, 0, 8)
+    strip_second_copies = exchange(second, 4, 1, send_d, recv_d)
     for a, b in SIDES:
         pl.semaphore_signal(here.at[0], inc=1, device_id=neighbour(2 * a, 2 * b, 0), device_id_type=MESH)
-    for cp in second_copies:
+
+    for cp in main_second:
         cp.wait_recv()
-
-    def unpack_second(j, carry):
-        for a in range(3):
-            vel[a, j + 1] = jnp.where(inside(j, a), whole(second, 4, a, j), 0.0)
-        pres[j] = whole(second, 4, 3, j)
-        return carry
-
-    loop(0, PLANES, unpack_second, 0, 11)
-    iteration(0, PLANES - 2)
-
-    lane_0 = lane_v == 0
+    unpack(unpack_second, 0, lambda a, j: second[a, j])
+    odd(0)
+    for cp in strip_second_copies:
+        cp.wait_recv()
+    unpack(unpack_second, 1, strip_second)
+    odd(1)
+
+    def joined(main, strip):
+        return jnp.where(lane_v < YLOW, pltpu.roll(strip, BY - SHIFT, 1), jnp.where(lane_v >= BY - YHIGH, strip, main))
 
     def last_pressure(i, total):
         j = i + LOW
-        vx = vel[0, j + 1, 0:BZ]
-        vz = vel[1, j + 1, 0:ROWS]
-        vy = vel[2, j + 1, 0:BZ]
-        rx = vel[0, j + 2, 0:BZ] - vx
-        rz = (pltpu.roll(vz, ROWS - 1, 0) - vz)[0:BZ]
-        next_y = jnp.where(lane_0, vel[2, j + 1, ROWS:ROWS + BZ], vy)
-        ry = pltpu.roll(next_y, BY - 1, 1) - vy
-        eta, div = viscosity(rx, rz, ry, pref[j, 0:BZ], expo[j, 0:BZ])
-        p = pres[j, 0:BZ] - PRESSURE_STEP * eta * div
+        parts = []
+        for part in range(2):
+            vx = vel[part, 0, j + 1, 0:BZ]
+            vz = vel[part, 1, j + 1]
+            vy = vel[part, 2, j + 1, 0:BZ]
+            rx = vel[part, 0, j + 2, 0:BZ] - vx
+            rz = (z_roll(vz, -1) - vz)[0:BZ]
+            ry = y_roll(vy, -1) - vy
+            eta, div = viscosity(rx, rz, ry, pref[part, j, 0:BZ], expo[part, j, 0:BZ])
+            parts.append((pres[part, j, 0:BZ] - PRESSURE_STEP * eta * div, eta))
+        p, eta = (joined(main, strip) for main, strip in zip(*parts))
         last_p[i] = p
         last_eta[i] = eta
         return total + p
@@ -344,10 +370,17 @@
         if n == 0:
             for a, b in SIDES:
                 pl.semaphore_signal(here.at[1], inc=1, device_id=neighbour(4 * a, 4 * b, 0), device_id_type=MESH)
-            iteration(1, PLANES - HIGH)
-            for a, comp in enumerate((0, 2, 1)):
-                out_v = vel.at[comp, pl.ds(LOW + 1, BX), pl.ds(0, BZ)]
-                cp = pltpu.make_async_copy(out_v, out_ref.at[a], out_sem.at[a])
+            even(0)
+            even(1)
+
+            def join(i, carry):
+                for a, comp in enumerate((0, 2, 1)):
+                    last_v[a, i] = joined(field(0, comp, i), field(1, comp, i))
+                return carry
+
+            loop(0, BX, join, 0, 8)
+            for a in range(3):
+                cp = pltpu.make_async_copy(last_v.at[a], out_ref.at[a], out_sem.at[a])
                 cp.start()
                 out_copies.append(cp)
         pltpu.make_async_copy(part, part, ar_recv.at[n]).wait()
@@ -361,7 +394,7 @@
     p_copy.start()
     out_copies.append(p_copy)
 
-    for cp in y_copies + main_copies + halo_copies + second_copies:
+    for cp in y_copies + main_copies + halo_copies + main_second + strip_second_copies:
         cp.wait_send()
     for cp in sum_sends + out_copies:
         cp.wait()
@@ -386,7 +419,7 @@
     f32 = jnp.float32
     hbm = pl.BlockSpec(memory_space=pltpu.HBM)
     dma = pltpu.SemaphoreType.DMA
-    plane = (2 * ROWS, BY)
+    planes = (2, PLANES, ROWS, BY)
     stacked = pl.pallas_call(
         functools.partial(kernel, sizes),
         out_shape=jax.ShapeDtypeStruct((5, BX, BZ, BY), f32),
@@ -401,17 +434,18 @@
             pltpu.VMEM((5, PLANES, ROWS, BY), f32),
             pltpu.VMEM((2, BX // 2, BZ, BY), f32),
             pltpu.VMEM((2, BX // 2, BZ, BY), f32),
-            pltpu.VMEM((3, PLANES + 2) + plane, f32),
-            pltpu.VMEM((PLANES,) + plane, f32),
-            pltpu.VMEM((PLANES,) + plane, f32),
-            pltpu.VMEM((PLANES,) + plane, f32),
-            pltpu.VMEM((PLANES,) + plane, f32),
+            pltpu.VMEM((2, 3, PLANES + 2, ROWS, BY), f32),
+            pltpu.VMEM(planes, f32),
+            pltpu.VMEM(planes, f32),
+            pltpu.VMEM(planes, f32),
+            pltpu.VMEM(planes, f32),
+            pltpu.VMEM((3, BX, BZ, BY), f32),
             pltpu.VMEM((BX, BZ, BY), f32),
             pltpu.VMEM((BX, BZ, BY), f32),
             pltpu.VMEM((2, 1, BY), f32),
             pltpu.VMEM((partners, 1, BY), f32),
             dma((8,)), dma((2,)), dma((2,)),
-            dma((8,)), dma((8,)), dma((8,)), dma((8,)), dma((8,)), dma((8,)),
+            dma((8,)), dma((8,)), dma((8,)), dma((8,)), dma((8,)), dma((8,)), dma((8,)), dma((8,)),
             dma((2,)), dma((2,)), dma((5,)), pltpu.SemaphoreType.REGULAR((2,)),
         ],
         name="stokes",

time: 63.7 us -> 62.3 us (0.978)
  Pallas kernels: 62.8 us -> 61.5 us
    pallas_call x1, Pallas kernels: 61.1 us -> 59.8 us  [local(): pl.pallas_call(functools.partial(kernel, sizes), out_shape=jax.ShapeDtype...]
where the time goes in v4:
time: 62.3 us; the launch traced here: 62.1 us
  Pallas kernels  61.5 us (99%)
  between operations  0.64 us (1%)
    pallas_call x1, Pallas kernels, local(): pl.pallas_call(functools.partial(kernel, sizes), out_shape=jax.ShapeDtype...  59.8 us
    pallas_call x1, Pallas kernels, local(): pl.pallas_call(split_kernel, out_shape=[jax.ShapeDtypeStruct((BX, BZ, BY)...  1.68 us

profile of v4, /device:TPU:1, one launch (start us, length us, event | category | flops | bytes accessed | tf_op | source)
XLA Modules:
  0.0 62.1 jit_solution(4057039956135251709)
XLA Ops:
  0.6 59.8 %stokes.1.in_ref = f32[5,16,8,128]{3,2,1,0:T(8,128)} custom-call(f32[16,8,128]{2,1,0:T(8,128)} %vx_ref.1, f32[16,8,128]{2,1,0:T(8,128)} %vy_ref.1, f32[16,8,128]{2,1,0:T(8,128)} %vz_ref.1, f32[16,8,128]{2,1,0:T(8,128)} %p_ref.1, s32[16,8,128]{2,1,0:T(8,128)} %ph_ref.1, f32[4]{0:T(128)} %vs_in.1, f32[4]{0:T(128)} %pn_in.1, f32[4]{0:T(128)} %dn_in.1), custom_call_target="tpu_custom_call" | custom-call | tf_op jit(solution)/shard_map/stokes/pallas_call | solution.py:423
  60.4 1.7 %split.1 = (f32[16,8,128]{2,1,0:T(8,128)}, f32[16,8,128]{2,1,0:T(8,128)}, f32[16,8,128]{2,1,0:T(8,128)}, f32[16,8,128]{2,1,0:T(8,128)}, f32[16,8,128]{2,1,0:T(8,128)}) custom-call(f32[5,16,8,128]{3,2,1,0:T(8,128)} %stokes.1.in_ref), custom_call_target="tpu_custom_call" | custom-call | tf_op jit(solution)/shard_map/split/pallas_call | solution.py:455

commit v5 on v4

--- a/solution.py
+++ b/solution.py
@@ -21,12 +21,13 @@
 ROWS = 2 * BZ
 GROUP = YLOW + YHIGH
 SHIFT = YHIGH + YLOW
+UNPACK = 11
 LEFT_AT, LEFT = 118, 30
 Z_LO = 4
 VMEM_BYTES = 62 * 1024 * 1024
 MESH = pl.DeviceIdType.MESH
 
-SIDES = tuple((a, b) for a in (-1, 0, 1) for b in (-1, 0, 1) if (a, b) != (0, 0))
+SIDES = ((-1, -1), (1, -1), (-1, 1), (1, 1), (-1, 0), (1, 0), (0, -1), (0, 1))
 
 
 def send_planes(a):
@@ -49,8 +50,11 @@
     assert (upper - lower) % unroll == 0
 
     def several(n, c):
+        stores = []
         for u in range(unroll):
-            c = body(lower + n * unroll + u, c)
+            c = body(lower + n * unroll + u, c, stores)
+        for ref, place, value in stores:
+            ref[place] = value
         return c
 
     return lax.fori_loop(0, (upper - lower) // unroll, several, carry)
@@ -118,26 +122,23 @@
 
 
     lane_v = lax.broadcasted_iota(jnp.int32, (BZ, BY), 1)
+    rows = pl.ds(0, BZ)
     for cp in in_copies:
         cp.wait()
     first[4, LOW:LOW + BX, 0:BZ] = ph_in[...].astype(jnp.float32)
 
-    def pack(k, carry):
+    def pack(k, carry, stores):
         lo = jnp.zeros((BZ, BY), jnp.float32)
         hi = jnp.zeros((BZ, BY), jnp.float32)
         for q in range(2):
             for a in range(5):
                 base = GROUP * a + 64 * q
-                rolled = first[a, LOW + 2 * k + q, 0:BZ]
-                if base:
-                    rolled = pltpu.roll(rolled, base, 1)
+                block = first[a, LOW + 2 * k + q, 0:BZ]
+                rolled = pltpu.roll(block, base, 1) if base else block
                 lo = jnp.where((lane_v >= base) & (lane_v < base + YHIGH), rolled, lo)
-                if base:
-                    hi = jnp.where((lane_v >= base - YLOW) & (lane_v < base), rolled, hi)
-                else:
-                    hi = jnp.where(lane_v >= BY - YLOW, rolled, hi)
-        s_pack[0, k] = lo
-        s_pack[1, k] = hi
+                rolled = pltpu.roll(block, base + SHIFT, 1)
+                hi = jnp.where((lane_v >= base + YHIGH) & (lane_v < base + SHIFT), rolled, hi)
+        stores += [(s_pack, (0, k), lo), (s_pack, (1, k), hi)]
         return carry
 
     loop(0, BX // 2, pack, 0, 4)
@@ -168,12 +169,10 @@
     for cp in y_copies:
         cp.wait_recv()
 
-    def unpack_y(k, carry):
-        low_lane = lax.rem(lane_v + YLOW, 64)
-        from_low = lax.rem(low_lane, GROUP) < YLOW
-        both = jnp.where(from_low, r_pack[1, k], r_pack[0, k])
-        first[5, LOW + 2 * k, 0:BZ] = both
-        first[5, LOW + 2 * k + 1, 0:BZ] = pltpu.roll(both, 64, 1)
+    def unpack_y(k, carry, stores):
+        both = jnp.where(lax.rem(lax.rem(lane_v, 64), GROUP) >= YHIGH, r_pack[1, k], r_pack[0, k])
+        stores.append((first, (5, LOW + 2 * k, rows), both))
+        stores.append((first, (5, LOW + 2 * k + 1, rows), pltpu.roll(both, 64, 1)))
         return carry
 
     loop(0, BX // 2, unpack_y, 0, 8)
@@ -191,9 +190,25 @@
         in_zy = in_z & (yi >= 0) & (yi < ngy * BY)
         masks.append({None: in_zy, 0: in_zy, 1: in_zy & (zi >= 1), 2: in_zy & (yi >= 1)})
 
-    def inside(part, j, comp):
-        xi = gx * BX - LOW + j
-        return masks[part][comp] & ((xi >= (1 if comp == 0 else 0)) & (xi < ngx * BX))
+    blank = jnp.zeros(full, jnp.float32)
+
+    def x_ends(part, viscous):
+        @pl.when(gx == 0)
+        def _():
+            for j in range(LOW):
+                for a in range(3):
+                    vel[part, a, j + 1] = blank
+                if viscous:
+                    pref[part, j] = blank
+            vel[part, 0, LOW + 1] = blank
+
+        @pl.when(gx == ngx - 1)
+        def _():
+            for j in range(LOW + BX, PLANES):
+                for a in range(3):
+                    vel[part, a, j + 1] = blank
+                if viscous:
+                    pref[part, j] = blank
 
     def splat(ref):
         return [jnp.full(full, ref[k], jnp.float32) for k in range(PHASES)]
@@ -207,43 +222,64 @@
             out = jnp.where(phase == float(k), table[k], out)
         return out
 
-    def unpack_first(part, j, whole):
+    def unpack_second(part, j, whole, stores):
         for a in range(3):
-            vel[part, a, j + 1] = jnp.where(inside(part, j, a), whole(a, j), 0.0)
-        pres[part, j] = whole(3, j)
-        phase = whole(4, j)
-        pref[part, j] = jnp.where(inside(part, j, None), select(phase, scales), 0.0)
-        expo[part, j] = select(phase, powers)
-        rho[part, j] = select(phase, densities)
-
-    def unpack_second(part, j, whole):
-        for a in range(3):
-            vel[part, a, j + 1] = jnp.where(inside(part, j, a), whole(a, j), 0.0)
-        pres[part, j] = whole(3, j)
-
-    def strip_first(a, j):
-        main = first[a, j]
-        halo = first[5, j]
-        if a:
-            halo = pltpu.roll(halo, BY - GROUP * a, 1)
-        low = pltpu.roll(jnp.where(lane >= BY - YLOW, halo, main), SHIFT, 1)
-        return jnp.where(lane < YHIGH, halo, jnp.where(lane < BY // 2, low, main))
-
-    def strip_second(a, j):
-        packed = second[4, j]
-        return pltpu.roll(packed, BY - LEFT * a, 1) if a else packed
-
-    def unpack(function, part, whole):
-        def body(j, carry):
-            function(part, j, whole)
+            stores.append((vel, (part, a, j + 1), jnp.where(masks[part][a], whole(a, j), 0.0)))
+        stores.append((pres, (part, j), whole(3, j)))
+
+    def lookups(part, j, phase, stores):
+        stores.append((pref, (part, j), jnp.where(masks[part][None], select(phase, scales), 0.0)))
+        stores.append((expo, (part, j), select(phase, powers)))
+        stores.append((rho, (part, j), select(phase, densities)))
+
+    def main_first(j, carry, stores):
+        unpack_second(0, j, lambda a, j: first[a, j], stores)
+        lookups(0, j, first[4, j], stores)
+        return carry
+
+    def main_again(j, carry, stores):
+        unpack_second(0, j, lambda a, j: second[a, j], stores)
+        return carry
+
+    def strip_own(j, carry, stores):
+        for a in range(5):
+            main = first[a, j]
+            own = jnp.where(lane < BY // 2, pltpu.roll(main, SHIFT, 1), main)
+            if a < 3:
+                stores.append((vel, (1, a, j + 1), own))
+            else:
+                stores.append((pres if a == 3 else expo, (1, j), own))
+        return carry
+
+    def strip_halo(a):
+        def body(j, carry, stores):
+            halo = first[5, j]
+            if a:
+                halo = pltpu.roll(halo, BY - GROUP * a, 1)
+            halo = jnp.where(lane < SHIFT, halo, vel[1, a, j + 1] if a < 3 else pres[1, j] if a == 3 else expo[1, j])
+            if a < 3:
+                stores.append((vel, (1, a, j + 1), jnp.where(masks[1][a], halo, 0.0)))
+            elif a == 3:
+                stores.append((pres, (1, j), halo))
+            else:
+                lookups(1, j, halo, stores)
             return carry
 
-        loop(0, PLANES, body, 0, 11)
+        return body
+
+    def strip_again(j, carry, stores):
+        def left(a, j):
+            packed = second[4, j]
+            return pltpu.roll(packed, BY - LEFT * a, 1) if a else packed
+
+        unpack_second(1, j, left, stores)
+        return carry
+
+    def planes(body):
+        loop(0, PLANES, body, 0, UNPACK)
 
     def iteration(part, first_plane, last_plane):
-        zero = jnp.zeros(full, jnp.float32)
-
-        def stage(j, carry):
+        def stage(j, carry, stores):
             eta_m, tx_m, vz_m, vy_m, fzx_m, fyx_m, pz_m, py_m, az_m, ay_m, rho_m = carry
             vx, vz, vy = vel[part, 0, j + 1], vel[part, 1, j + 1], vel[part, 2, j + 1]
             rx = vel[part, 0, j + 2] - vx
@@ -251,13 +287,13 @@
             ry = y_roll(vy, -1) - vy
             eta, div = viscosity(rx, rz, ry, pref[part, j], expo[part, j])
             p = pres[part, j] - PRESSURE_STEP * eta * div
-            pres[part, j] = p
+            stores.append((pres, (part, j), p))
             tx, tz, ty = eta * rx - p, eta * rz - p, eta * ry - p
             ax = eta + eta_m
             az = eta + z_roll(eta, 1)
             ay = eta + y_roll(eta, 1)
-            exz = ax + z_roll(ax, 1)
-            exy = ax + y_roll(ax, 1)
+            exz = az + az_m
+            exy = ay + ay_m
             eyz = ay + z_roll(ay, 1)
             fzx = exz * (vz - vz_m)
             fyx = exy * (vy - vy_m)
@@ -266,16 +302,20 @@
             fyz = eyz * (vy - z_roll(vy, 1))
             fzy = eyz * (vz - y_roll(vz, 1))
             res = tx - tx_m + 0.25 * ((z_roll(fxz, -1) - fxz) + (y_roll(fxy, -1) - fxy))
-            vel[part, 0, j + 1] = jnp.where(inside(part, j, 0), vx + (2.0 * VELOCITY_STEP) * res / ax, 0.0)
+            new = jnp.where(masks[part][0], vx + (2.0 * VELOCITY_STEP) * res / ax, 0.0)
+            stores.append((vel, (part, 0, j + 1), new))
             res = pz_m + 0.25 * (fzx - fzx_m) - rho_m
-            vel[part, 1, j] = jnp.where(inside(part, j - 1, 1), vz_m + (2.0 * VELOCITY_STEP) * res / az_m, 0.0)
+            new = jnp.where(masks[part][1], vz_m + (2.0 * VELOCITY_STEP) * res / az_m, 0.0)
+            stores.append((vel, (part, 1, j), new))
             res = py_m + 0.25 * (fyx - fyx_m)
-            vel[part, 2, j] = jnp.where(inside(part, j - 1, 2), vy_m + (2.0 * VELOCITY_STEP) * res / ay_m, 0.0)
+            new = jnp.where(masks[part][2], vy_m + (2.0 * VELOCITY_STEP) * res / ay_m, 0.0)
+            stores.append((vel, (part, 2, j), new))
             pz = tz - z_roll(tz, 1) + 0.25 * (y_roll(fzy, -1) - fzy)
             py = ty - y_roll(ty, 1) + 0.25 * (z_roll(fyz, -1) - fyz)
             return eta, tx, vz, vy, fzx, fyx, pz, py, az, ay, rho[part, j]
 
-        loop(first_plane, last_plane + 1, stage, (zero,) * 11, (last_plane + 1 - first_plane) // 3)
+        loop(first_plane, last_plane + 1, stage, (blank,) * 11, (last_plane + 1 - first_plane) // 3)
+        x_ends(part, False)
 
     def odd(part):
         iteration(part, 0, PLANES - 2)
@@ -288,31 +328,35 @@
 
     for cp in main_copies:
         cp.wait_recv()
-    unpack(unpack_first, 0, lambda a, j: first[a, j])
+    planes(main_first)
+    x_ends(0, True)
     odd(0)
     even(0)
 
-    def repack_main(i, carry):
+    def repack_main(i, carry, stores):
         for a in range(4):
-            second[a, i + LOW, 0:BZ] = field(0, a, i)
+            stores.append((second, (a, i + LOW, rows), field(0, a, i)))
         return carry
 
     loop(0, BX, repack_main, 0, 8)
     main_second = exchange(second, 0, 4, send_c, recv_c)
+    planes(strip_own)
 
     for cp in halo_copies:
         cp.wait_recv()
-    unpack(unpack_first, 1, strip_first)
+    for a in range(5):
+        planes(strip_halo(a))
+    x_ends(1, True)
     odd(1)
     even(1)
 
-    def repack_strip(i, carry):
+    def repack_strip(i, carry, stores):
         packed = field(1, 0, i)
         place = lane_v + jnp.where(lane_v >= LEFT_AT, -LEFT_AT, BY - LEFT_AT)
         for a in range(1, 4):
             rolled = pltpu.roll(field(1, a, i), LEFT * a, 1)
             packed = jnp.where((place >= LEFT * a) & (place < LEFT * (a + 1)), rolled, packed)
-        second[4, i + LOW, 0:BZ] = packed
+        stores.append((second, (4, i + LOW, rows), packed))
         return carry
 
     loop(0, BX, repack_strip, 0, 8)
@@ -322,17 +366,19 @@
 
     for cp in main_second:
         cp.wait_recv()
-    unpack(unpack_second, 0, lambda a, j: second[a, j])
+    planes(main_again)
+    x_ends(0, False)
     odd(0)
     for cp in strip_second_copies:
         cp.wait_recv()
-    unpack(unpack_second, 1, strip_second)
+    planes(strip_again)
+    x_ends(1, False)
     odd(1)
 
     def joined(main, strip):
         return jnp.where(lane_v < YLOW, pltpu.roll(strip, BY - SHIFT, 1), jnp.where(lane_v >= BY - YHIGH, strip, main))
 
-    def last_pressure(i, total):
+    def last_pressure(i, total, stores):
         j = i + LOW
         parts = []
         for part in range(2):
@@ -345,8 +391,7 @@
             eta, div = viscosity(rx, rz, ry, pref[part, j, 0:BZ], expo[part, j, 0:BZ])
             parts.append((pres[part, j, 0:BZ] - PRESSURE_STEP * eta * div, eta))
         p, eta = (joined(main, strip) for main, strip in zip(*parts))
-        last_p[i] = p
-        last_eta[i] = eta
+        stores += [(last_p, i, p), (last_eta, i, eta)]
         return total + p
 
     total = loop(0, BX, last_pressure, jnp.zeros((BZ, BY), jnp.float32), 8)
@@ -373,9 +418,9 @@
             even(0)
             even(1)
 
-            def join(i, carry):
+            def join(i, carry, stores):
                 for a, comp in enumerate((0, 2, 1)):
-                    last_v[a, i] = joined(field(0, comp, i), field(1, comp, i))
+                    stores.append((last_v, (a, i), joined(field(0, comp, i), field(1, comp, i))))
                 return carry
 
             loop(0, BX, join, 0, 8)

time: 62.3 us -> 60.5 us (0.971)
  Pallas kernels: 61.5 us -> 59.6 us
    pallas_call x1, Pallas kernels: 59.8 us -> 57.9 us  [local(): pl.pallas_call(functools.partial(kernel, sizes), out_shape=jax.ShapeDtype...]
where the time goes in v5:
time: 60.5 us; the launch traced here: 60.2 us
  Pallas kernels  59.6 us (99%)
  between operations  0.64 us (1%)
    pallas_call x1, Pallas kernels, local(): pl.pallas_call(functools.partial(kernel, sizes), out_shape=jax.ShapeDtype...  57.9 us
    pallas_call x1, Pallas kernels, local(): pl.pallas_call(split_kernel, out_shape=[jax.ShapeDtypeStruct((BX, BZ, BY)...  1.68 us

profile of v5, /device:TPU:1, one launch (start us, length us, event | category | flops | bytes accessed | tf_op | source)
XLA Modules:
  0.0 60.2 jit_solution(17034007210375778258)
XLA Ops:
  0.6 57.9 %stokes.1.in_ref = f32[5,16,8,128]{3,2,1,0:T(8,128)} custom-call(f32[16,8,128]{2,1,0:T(8,128)} %vx_ref.1, f32[16,8,128]{2,1,0:T(8,128)} %vy_ref.1, f32[16,8,128]{2,1,0:T(8,128)} %vz_ref.1, f32[16,8,128]{2,1,0:T(8,128)} %p_ref.1, s32[16,8,128]{2,1,0:T(8,128)} %ph_ref.1, f32[4]{0:T(128)} %vs_in.1, f32[4]{0:T(128)} %pn_in.1, f32[4]{0:T(128)} %dn_in.1), custom_call_target="tpu_custom_call" | custom-call | tf_op jit(solution)/shard_map/stokes/pallas_call | solution.py:468
  58.5 1.7 %split.1 = (f32[16,8,128]{2,1,0:T(8,128)}, f32[16,8,128]{2,1,0:T(8,128)}, f32[16,8,128]{2,1,0:T(8,128)}, f32[16,8,128]{2,1,0:T(8,128)}, f32[16,8,128]{2,1,0:T(8,128)}) custom-call(f32[5,16,8,128]{3,2,1,0:T(8,128)} %stokes.1.in_ref), custom_call_target="tpu_custom_call" | custom-call | tf_op jit(solution)/shard_map/split/pallas_call | solution.py:500

commit v6 on v5

--- a/solution.py
+++ b/solution.py
@@ -77,8 +77,8 @@
 
 
 def kernel(sizes, vx_ref, vy_ref, vz_ref, p_ref, ph_ref, vs_in, pn_in, dn_in, out_ref,
-           vs_ref, pn_ref, dn_ref, ph_in, first, second, s_pack, r_pack, vel, pres, pref, expo, rho, last_v, last_p, last_eta, ar_src, ar_buf,
-           in_sem, ysend, yrecv, send_a, recv_a, send_b, recv_b, send_c, recv_c, send_d, recv_d, ar_send, ar_recv, out_sem, here):
+           vs_ref, pn_ref, dn_ref, ph_in, first, second, s_pack, r_pack, vel, pres, pref, expo, rho, ar_src, ar_buf,
+           in_sem, ysend, yrecv, send_a, recv_a, send_b, recv_b, send_c, recv_c, send_d, recv_d, ar_send, ar_recv, here):
     ngx, ngy, ngz, z_lo = sizes
     gx, gy, gz = lax.axis_index("gx"), lax.axis_index("gy"), lax.axis_index("gz")
 
@@ -314,7 +314,7 @@
             py = ty - y_roll(ty, 1) + 0.25 * (z_roll(fyz, -1) - fyz)
             return eta, tx, vz, vy, fzx, fyx, pz, py, az, ay, rho[part, j]
 
-        loop(first_plane, last_plane + 1, stage, (blank,) * 11, (last_plane + 1 - first_plane) // 3)
+        loop(first_plane, last_plane + 1, stage, (blank,) * 11, last_plane + 1 - first_plane)
         x_ends(part, False)
 
     def odd(part):
@@ -391,15 +391,12 @@
             eta, div = viscosity(rx, rz, ry, pref[part, j, 0:BZ], expo[part, j, 0:BZ])
             parts.append((pres[part, j, 0:BZ] - PRESSURE_STEP * eta * div, eta))
         p, eta = (joined(main, strip) for main, strip in zip(*parts))
-        stores += [(last_p, i, p), (last_eta, i, eta)]
+        stores += [(out_ref, (3, i), p), (out_ref, (4, i), eta)]
         return total + p
 
     total = loop(0, BX, last_pressure, jnp.zeros((BZ, BY), jnp.float32), 8)
 
     total = jnp.sum(total, axis=0, keepdims=True)
-    eta_copy = pltpu.make_async_copy(last_eta, out_ref.at[4], out_sem.at[4])
-    eta_copy.start()
-    out_copies = [eta_copy]
     base = 0
     sum_sends = []
     for n, devices in enumerate(sum_phases):
@@ -420,41 +417,30 @@
 
             def join(i, carry, stores):
                 for a, comp in enumerate((0, 2, 1)):
-                    stores.append((last_v, (a, i), joined(field(0, comp, i), field(1, comp, i))))
+                    stores.append((out_ref, (a, i), joined(field(0, comp, i), field(1, comp, i))))
                 return carry
 
             loop(0, BX, join, 0, 8)
-            for a in range(3):
-                cp = pltpu.make_async_copy(last_v.at[a], out_ref.at[a], out_sem.at[a])
-                cp.start()
-                out_copies.append(cp)
         pltpu.make_async_copy(part, part, ar_recv.at[n]).wait()
         for o in range(count):
             total = total + ar_buf[base + o]
         base += count
     cells = float(ngx * ngy * ngz * BX * BZ * BY)
     mean = jnp.sum(total) / cells
-    last_p[...] = last_p[...] - mean
-    p_copy = pltpu.make_async_copy(last_p, out_ref.at[3], out_sem.at[3])
-    p_copy.start()
-    out_copies.append(p_copy)
+    out_ref[3] = out_ref[3] - mean
 
     for cp in y_copies + main_copies + halo_copies + main_second + strip_second_copies:
         cp.wait_send()
-    for cp in sum_sends + out_copies:
+    for cp in sum_sends:
         cp.wait()
 
 
 def split_kernel(in_ref, *refs):
-    *outs, held, sem_in, sem_out = refs
-    into = [pltpu.make_async_copy(in_ref.at[n], held.at[n], sem_in.at[n]) for n in range(5)]
-    back = [pltpu.make_async_copy(held.at[n], out, sem_out.at[n]) for n, out in enumerate(outs)]
-    for cp in into:
+    *outs, sem = refs
+    copies = [pltpu.make_async_copy(in_ref.at[n], out, sem.at[n]) for n, out in enumerate(outs)]
+    for cp in copies:
         cp.start()
-    for cp, after in zip(into, back):
-        cp.wait()
-        after.start()
-    for cp in back:
+    for cp in copies:
         cp.wait()
 
 
@@ -467,9 +453,9 @@
     planes = (2, PLANES, ROWS, BY)
     stacked = pl.pallas_call(
         functools.partial(kernel, sizes),
-        out_shape=jax.ShapeDtypeStruct((5, BX, BZ, BY), f32),
+        out_shape=pltpu.VMEM((5, BX, BZ, BY), f32),
         in_specs=[hbm] * 8,
-        out_specs=hbm,
+        out_specs=pl.BlockSpec(memory_space=pltpu.VMEM),
         scratch_shapes=[
             pltpu.SMEM((PHASES,), f32),
             pltpu.SMEM((PHASES,), f32),
@@ -484,14 +470,11 @@
             pltpu.VMEM(planes, f32),
             pltpu.VMEM(planes, f32),
             pltpu.VMEM(planes, f32),
-            pltpu.VMEM((3, BX, BZ, BY), f32),
-            pltpu.VMEM((BX, BZ, BY), f32),
-            pltpu.VMEM((BX, BZ, BY), f32),
             pltpu.VMEM((2, 1, BY), f32),
             pltpu.VMEM((partners, 1, BY), f32),
             dma((8,)), dma((2,)), dma((2,)),
             dma((8,)), dma((8,)), dma((8,)), dma((8,)), dma((8,)), dma((8,)), dma((8,)), dma((8,)),
-            dma((2,)), dma((2,)), dma((5,)), pltpu.SemaphoreType.REGULAR((2,)),
+            dma((2,)), dma((2,)), pltpu.SemaphoreType.REGULAR((2,)),
         ],
         name="stokes",
         compiler_params=pltpu.CompilerParams(
@@ -500,11 +483,11 @@
     return pl.pallas_call(
         split_kernel,
         out_shape=[jax.ShapeDtypeStruct((BX, BZ, BY), f32)] * 5,
-        in_specs=[hbm],
+        in_specs=[pl.BlockSpec(memory_space=pl.ANY)],
         out_specs=[hbm] * 5,
-        scratch_shapes=[pltpu.VMEM((5, BX, BZ, BY), f32), dma((5,)), dma((5,))],
+        scratch_shapes=[dma((5,))],
         name="split",
-        compiler_params=pltpu.CompilerParams(vmem_limit_bytes=VMEM_BYTES),
+        compiler_params=pltpu.CompilerParams(vmem_limit_bytes=2 * 1024 * 1024),
     )(stacked)
 
 

time: 60.5 us -> 58.3 us (0.964)
  Pallas kernels: 59.6 us -> 57.4 us
    pallas_call x1, Pallas kernels: 57.9 us -> 56.7 us  [local(): pl.pallas_call(functools.partial(kernel, sizes), out_shape=pltpu.VMEM((5,...]
    pallas_call x1, Pallas kernels: 1.68 us -> 0.76 us  [local(): pl.pallas_call(split_kernel, out_shape=[jax.ShapeDtypeStruct((BX, BZ, BY)...]
where the time goes in v6:
time: 58.3 us; the launch traced here: 58.1 us
  Pallas kernels  57.4 us (98%)
  between operations  0.64 us (1%)
    pallas_call x1, Pallas kernels, local(): pl.pallas_call(functools.partial(kernel, sizes), out_shape=pltpu.VMEM((5,...  56.7 us

profile of v6, /device:TPU:1, one launch (start us, length us, event | category | flops | bytes accessed | tf_op | source)
XLA Modules:
  0.0 58.1 jit_solution(5873396293714276166)
XLA Ops:
  0.6 56.7 %stokes.1.in_ref = f32[5,16,8,128]{3,2,1,0:T(8,128)S(1)} custom-call(f32[16,8,128]{2,1,0:T(8,128)} %vx_ref.1, f32[16,8,128]{2,1,0:T(8,128)} %vy_ref.1, f32[16,8,128]{2,1,0:T(8,128)} %vz_ref.1, f32[16,8,128]{2,1,0:T(8,128)} %p_ref.1, s32[16,8,128]{2,1,0:T(8,128)} %ph_ref.1, f32[4]{0:T(128)} %vs_in.1, f32[4]{0:T(128)} %pn_in.1, f32[4]{0:T(128)} %dn_in.1), custom_call_target="tpu_custom_call" | custom-call | tf_op jit(solution)/shard_map/stokes/pallas_call | solution.py:454
  57.3 0.8 %split.1 = (f32[16,8,128]{2,1,0:T(8,128)}, f32[16,8,128]{2,1,0:T(8,128)}, f32[16,8,128]{2,1,0:T(8,128)}, f32[16,8,128]{2,1,0:T(8,128)}, f32[16,8,128]{2,1,0:T(8,128)}) custom-call(f32[5,16,8,128]{3,2,1,0:T(8,128)S(1)} %stokes.1.in_ref), custom_call_target="tpu_custom_call" | custom-call | tf_op jit(solution)/shard_map/split/pallas_call | solution.py:483

commit v7 on v6

--- a/solution.py
+++ b/solution.py
@@ -21,7 +21,7 @@
 ROWS = 2 * BZ
 GROUP = YLOW + YHIGH
 SHIFT = YHIGH + YLOW
-UNPACK = 11
+UNPACK = 22
 LEFT_AT, LEFT = 118, 30
 Z_LO = 4
 VMEM_BYTES = 62 * 1024 * 1024
@@ -77,7 +77,7 @@
 
 
 def kernel(sizes, vx_ref, vy_ref, vz_ref, p_ref, ph_ref, vs_in, pn_in, dn_in, out_ref,
-           vs_ref, pn_ref, dn_ref, ph_in, first, second, s_pack, r_pack, vel, pres, pref, expo, rho, ar_src, ar_buf,
+           vs_ref, pn_ref, dn_ref, ph_in, first, second, s_pack, r_pack, vel, pres, pref, expo, rho, last, ar_src, ar_buf,
            in_sem, ysend, yrecv, send_a, recv_a, send_b, recv_b, send_c, recv_c, send_d, recv_d, ar_send, ar_recv, here):
     ngx, ngy, ngz, z_lo = sizes
     gx, gy, gz = lax.axis_index("gx"), lax.axis_index("gy"), lax.axis_index("gz")
@@ -326,6 +326,24 @@
     def field(part, a, i):
         return vel[part, a, i + LOW + 1, 0:BZ] if a < 3 else pres[part, i + LOW, 0:BZ]
 
+    counted = ((lane_v >= YLOW) & (lane_v < BY - YHIGH), (lane_v >= BY - YHIGH) | ((lane_v >= SHIFT) & (lane_v < SHIFT + YLOW)))
+
+    def last_pressure(part):
+        def body(i, total, stores):
+            j = i + LOW
+            vx = vel[part, 0, j + 1, 0:BZ]
+            vz = vel[part, 1, j + 1]
+            vy = vel[part, 2, j + 1, 0:BZ]
+            rx = vel[part, 0, j + 2, 0:BZ] - vx
+            rz = (z_roll(vz, -1) - vz)[0:BZ]
+            ry = y_roll(vy, -1) - vy
+            eta, div = viscosity(rx, rz, ry, pref[part, j, 0:BZ], expo[part, j, 0:BZ])
+            p = pres[part, j, 0:BZ] - PRESSURE_STEP * eta * div
+            stores += [(last, (part, 0, i), p), (last, (part, 1, i), eta)]
+            return total + jnp.where(counted[part], p, 0.0)
+
+        return body
+
     for cp in main_copies:
         cp.wait_recv()
     planes(main_first)
@@ -369,6 +387,7 @@
     planes(main_again)
     x_ends(0, False)
     odd(0)
+    total = loop(0, BX, last_pressure(0), jnp.zeros((BZ, BY), jnp.float32), BX)
     for cp in strip_second_copies:
         cp.wait_recv()
     planes(strip_again)
@@ -378,24 +397,7 @@
     def joined(main, strip):
         return jnp.where(lane_v < YLOW, pltpu.roll(strip, BY - SHIFT, 1), jnp.where(lane_v >= BY - YHIGH, strip, main))
 
-    def last_pressure(i, total, stores):
-        j = i + LOW
-        parts = []
-        for part in range(2):
-            vx = vel[part, 0, j + 1, 0:BZ]
-            vz = vel[part, 1, j + 1]
-            vy = vel[part, 2, j + 1, 0:BZ]
-            rx = vel[part, 0, j + 2, 0:BZ] - vx
-            rz = (z_roll(vz, -1) - vz)[0:BZ]
-            ry = y_roll(vy, -1) - vy
-            eta, div = viscosity(rx, rz, ry, pref[part, j, 0:BZ], expo[part, j, 0:BZ])
-            parts.append((pres[part, j, 0:BZ] - PRESSURE_STEP * eta * div, eta))
-        p, eta = (joined(main, strip) for main, strip in zip(*parts))
-        stores += [(out_ref, (3, i), p), (out_ref, (4, i), eta)]
-        return total + p
-
-    total = loop(0, BX, last_pressure, jnp.zeros((BZ, BY), jnp.float32), 8)
-
+    total = loop(0, BX, last_pressure(1), total, BX)
     total = jnp.sum(total, axis=0, keepdims=True)
     base = 0
     sum_sends = []
@@ -418,6 +420,8 @@
             def join(i, carry, stores):
                 for a, comp in enumerate((0, 2, 1)):
                     stores.append((out_ref, (a, i), joined(field(0, comp, i), field(1, comp, i))))
+                for a in range(2):
+                    stores.append((out_ref, (a + 3, i), joined(last[0, a, i], last[1, a, i])))
                 return carry
 
             loop(0, BX, join, 0, 8)
@@ -470,6 +474,7 @@
             pltpu.VMEM(planes, f32),
             pltpu.VMEM(planes, f32),
             pltpu.VMEM(planes, f32),
+            pltpu.VMEM((2, 2, BX, BZ, BY), f32),
             pltpu.VMEM((2, 1, BY), f32),
             pltpu.VMEM((partners, 1, BY), f32),
             dma((8,)), dma((2,)), dma((2,)),

time: 58.3 us -> 58 us (level)
  no operation moved by 1% of the time
where the time goes in v7:
time: 58 us; the launch traced here: 57.8 us
  Pallas kernels  57.1 us (98%)
  between operations  0.64 us (1%)
    pallas_call x1, Pallas kernels, local(): pl.pallas_call(functools.partial(kernel, sizes), out_shape=pltpu.VMEM((5,...  56.4 us

profile of v7, /device:TPU:1, one launch (start us, length us, event | category | flops | bytes accessed | tf_op | source)
XLA Modules:
  0.0 57.8 jit_solution(13977003992890107510)
XLA Ops:
  0.6 56.4 %stokes.1.in_ref = f32[5,16,8,128]{3,2,1,0:T(8,128)S(1)} custom-call(f32[16,8,128]{2,1,0:T(8,128)} %vx_ref.1, f32[16,8,128]{2,1,0:T(8,128)} %vy_ref.1, f32[16,8,128]{2,1,0:T(8,128)} %vz_ref.1, f32[16,8,128]{2,1,0:T(8,128)} %p_ref.1, s32[16,8,128]{2,1,0:T(8,128)} %ph_ref.1, f32[4]{0:T(128)} %vs_in.1, f32[4]{0:T(128)} %pn_in.1, f32[4]{0:T(128)} %dn_in.1), custom_call_target="tpu_custom_call" | custom-call | tf_op jit(solution)/shard_map/stokes/pallas_call | solution.py:458
  57.0 0.8 %split.1 = (f32[16,8,128]{2,1,0:T(8,128)}, f32[16,8,128]{2,1,0:T(8,128)}, f32[16,8,128]{2,1,0:T(8,128)}, f32[16,8,128]{2,1,0:T(8,128)}, f32[16,8,128]{2,1,0:T(8,128)}) custom-call(f32[5,16,8,128]{3,2,1,0:T(8,128)S(1)} %stokes.1.in_ref), custom_call_target="tpu_custom_call" | custom-call | tf_op jit(solution)/shard_map/split/pallas_call | solution.py:488
